TPU v7x, 32 devices: a whole 2x2x4 slice. The times are simulated.
32 devices in a mesh: grp: 2 (over x), space: 16 (over z, y, core).
Axes of the slice: x: 2, y: 2, z: 4, core: 2. Of those that a mesh axis runs over, the one named last changes fastest.
Arguments:
- right_side: float32 [165, 12288], P(None, ('grp', 'space')), parts along dimension 1, may hold values from -48 to 48
- capacity: float32 [12288], P(('grp', 'space')), parts along dimension 0, may hold values from 0.5 to 2
- base_cond: float32 [192, 24, 4096], P(('grp', 'space')), parts along dimension 0, may hold values from 0.0005 to 0.005
- var_field: float32 [8, 12288], P(None, ('grp', 'space')), parts along dimension 1, may hold values from -1 to 1
- block_cols: int32 [192, 23], P(('grp', 'space')), parts along dimension 0, may hold values from 0 to 11, as said below
- send_list: int32 [32, 2, 3], P(('grp', 'space')), parts along dimension 0, may hold values from 0 to 5, as said below
Outputs:
- solution_field: float32 [165, 12288], P(None, ('grp', 'space')), parts along dimension 1
- residual: float32 [165, 12288], P(None, ('grp', 'space')), parts along dimension 1
There are 2 independent parts, one for each index of `grp`. A program takes and returns all parts, laid end to end along the dimension named above; each array names one. Nothing has to cross between parts.
Inputs may be any that keep to these rules, and one draw needn't show every extreme that they name: `block_cols`: A value below 6 names a block of the same device; 6 + h names the h-th block that the previous device of space sends up, 9 + h the h-th block that the next device sends down. The first device never names the previous one, the last never names the next one; every other value occurs on every device. `send_list`: on every device the 6 blocks differ; block 5 is always sent up and block 0 always sent down.
All inputs are finite; a program needn't handle non-finite values.
Results may differ from a plain program's by a relative error of at most 0.0003.
Values sent between devices are 32-bit elements; how exact they have to be, the bound alone decides.
A program may use at most 128 MiB of HBM per device.

v0:
```python
import functools
import math

import jax
import jax.numpy as jnp
import numpy as np
from jax import lax
from jax.experimental import pallas as pl
from jax.experimental.pallas import tpu as pltpu
from jax.sharding import PartitionSpec as P

VARS = 8
ORDER = 3
ITERS = 2
SPREAD = 0.14
ROWS = 176
HALF = ROWS // 2
MSG = ROWS + HALF
MESH = pl.DeviceIdType.MESH
F32 = jnp.float32
BF16 = jnp.bfloat16


def chaos_tables():
    entries = []

    def grow(prefix, left):
        if len(prefix) == VARS:
            entries.append(tuple(prefix))
            return
        for degree in range(left + 1):
            grow(prefix + [degree], left - degree)

    grow([], ORDER)
    entries.sort(key=lambda m: (sum(m), tuple(-v for v in m)))
    lookup = {m: i for i, m in enumerate(entries)}
    coupling = np.zeros((VARS, ROWS, ROWS), np.float32)
    scale = np.ones((ROWS,), np.float64)
    for i, m in enumerate(entries):
        scale[i] = math.sqrt(math.prod(math.factorial(v) for v in m))
        for k in range(VARS):
            if m[k] > 0:
                coupling[k, i, lookup[m[:k] + (m[k] - 1,) + m[k + 1 :]]] = m[k]
            raised = m[:k] + (m[k] + 1,) + m[k + 1 :]
            if raised in lookup:
                coupling[k, i, lookup[raised]] = 1.0
    scales = np.stack([scale, 1.0 / scale**2, 1.0 / scale], 0)
    return coupling, np.broadcast_to(scales[:, :, None], (3, ROWS, 128)).astype(np.float32)


def split2(x):
    hi = x.astype(BF16)
    return hi, (x - hi.astype(F32)).astype(BF16)


def split3(x):
    hi = x.astype(BF16)
    rest = x - hi.astype(F32)
    mid = rest.astype(BF16)
    return hi, mid, (rest - mid.astype(F32)).astype(BF16)


def nn(a, b):
    return lax.dot_general(a, b, (((1,), (0,)), ((), ())), preferred_element_type=F32)


def nt(a, b):
    return lax.dot_general(a, b, (((1,), (1,)), ((), ())), preferred_element_type=F32)


def swap(x):
    return pltpu.roll(x, 64, 1)


def wide(x):
    return jnp.concatenate([x, x, x], axis=1)


def kernel(
    n,
    rhs_ref, var_ref, cap_ref, codes_ref, coup_ref, scale_ref, base_ref,
    x_ref, r_ref,
    inp, base, wc, wf, whi, wlo, ybuf, ext, lam, dmode, fieldb, gamb, cplb, qb, r1b, accb,
    fs, fr, hs, hr, ts, tr, allb,
    base_sem, send_sem, recv_sem, all_send, all_recv,
):
    me = lax.axis_index("space")
    prev, nxt = lax.rem(me + n - 1, n), lax.rem(me + 1, n)
    chunk = base.shape[1] // 4

    def base_copy(i):
        cols = pl.ds(i * chunk, chunk)
        return pltpu.make_async_copy(base_ref.at[:, cols], base.at[:, cols], base_sem.at[i])

    for i in range(4):
        base_copy(i).start()

    barrier = pltpu.get_barrier_semaphore()

    def greet(i, c):
        pl.semaphore_signal(
            barrier, inc=1, device_id={"space": lax.rem(me + i, n)}, device_id_type=MESH
        )
        return c

    lax.fori_loop(1, n, greet, 0)

    def remote(src, dst, which, peer):
        return pltpu.make_async_remote_copy(
            src_ref=src, dst_ref=dst, send_sem=send_sem.at[which], recv_sem=recv_sem.at[which],
            device_id={"space": peer}, device_id_type=MESH,
        )

    def pair(src, dst, e):
        up = remote(src.at[0], dst.at[0], 2 * e, nxt)
        down = remote(src.at[1], dst.at[1], 2 * e + 1, prev)
        return up, down

    def send(up, down):
        @pl.when(me < n - 1)
        def _():
            up.start()

        @pl.when(me > 0)
        def _():
            down.start()

    def arrive(up, down):
        @pl.when(me > 0)
        def _():
            up.wait_recv()

        @pl.when(me < n - 1)
        def _():
            down.wait_recv()

    def sent(up, down):
        @pl.when(me < n - 1)
        def _():
            up.wait_send()

        @pl.when(me > 0)
        def _():
            down.wait_send()

    def left_mask(rows):
        return lax.broadcasted_iota(jnp.int32, (rows, 128), 1) < 64

    def pack(dst, first, middle, last):
        rows = first.shape[0]
        half = rows // 2
        left = left_mask(half)
        top, low = middle[:half], middle[half:]
        dst[0, 0:rows] = first
        dst[0, rows : rows + half] = jnp.where(left, top, swap(low))
        dst[1, 0:rows] = last
        dst[1, rows : rows + half] = jnp.where(left, swap(top), low)

    def unpack(src, rows):
        half = rows // 2
        left = left_mask(half)
        up, down = src[0, rows : rows + half], src[1, rows : rows + half]
        middle = jnp.concatenate(
            [jnp.where(left, up, swap(down)), jnp.where(left, swap(up), down)], axis=0
        )
        return src[0, 0:rows], middle, src[1, 0:rows]

    @pl.when(me == 0)
    def _():
        for buf in (fr.at[0], fr.at[1], hr.at[0], hr.at[1], tr):
            buf[0] = jnp.zeros(buf.shape[1:], F32)

    @pl.when(me == n - 1)
    def _():
        for buf in (fr.at[0], fr.at[1], hr.at[0], hr.at[1], tr):
            buf[1] = jnp.zeros(buf.shape[1:], F32)

    terms = rhs_ref.shape[0]
    nodes = rhs_ref.shape[1]
    inp[...] = jnp.zeros_like(inp)
    inp[0:terms] = rhs_ref[...]
    inp[ROWS : ROWS + 8] = var_ref[...]
    inp[ROWS + 8 : ROWS + 9] = cap_ref[...]
    order = (
        lax.broadcasted_iota(jnp.int32, (nodes, nodes), 0) == codes_ref[0:1, 0:nodes]
    ).astype(F32).astype(BF16)
    h, m, l = split3(inp[...])
    moved = nn(h, order) + (nn(m, order) + nn(l, order))
    fieldb[...] = moved[:ROWS] * wide(scale_ref[0])
    lam[0:8] = moved[ROWS : ROWS + 8] * SPREAD
    lam[8:9] = jnp.ones((1, nodes), F32)
    lam[9:16] = jnp.zeros((7, nodes), F32)
    cap = moved[ROWS + 8 : ROWS + 9]

    pl.semaphore_wait(barrier, n - 1)

    def send_field(i, x):
        pack(fs.at[i], x[:, 0:128], x[:, 128:256], x[:, 256:384])
        send(*pair(fs.at[i], fr.at[i], i))

    send_field(0, fieldb[...])

    def couple_first():
        h, l = split2(fieldb[...])
        accb[...] = fieldb[...]

        def step(k, c):
            y = nn(coup_ref[k], h) + nn(coup_ref[k], l)
            ybuf[k] = y
            accb[...] += lam[pl.ds(k, 1)] * y
            return c

        lax.fori_loop(0, VARS, step, 0)
        gamb[...] = accb[...]

    couple_first()

    rowsc, rowse = wc.shape[0], base.shape[0]
    pick = (
        lax.broadcasted_iota(jnp.int32, (rowsc, rowse), 0) == codes_ref[0:1, 384 : 384 + rowse]
    ).astype(F32).astype(BF16)
    for i in range(4):
        base_copy(i).wait()

        def merge(j, c):
            cols = pl.ds(pl.multiple_of(i * chunk + j * 512, 512), 512)
            h, l = split2(base[:, cols])
            wc[:, cols] = nn(pick, h) + nn(pick, l)
            return c

        lax.fori_loop(0, chunk // 512, merge, 0)
    left8 = left_mask(8)

    def lay(j, c):
        cols = pl.ds(pl.multiple_of(j * 128, 128), 128)
        for t in range(6):
            even = wc[t * 16 : t * 16 + 8, cols]
            odd = wc[t * 16 + 8 : t * 16 + 16, cols]
            wf[pl.ds(t * 64 + 2 * j, 8, stride=nodes), :] = jnp.where(left8, even, swap(odd))
            wf[pl.ds(t * 64 + 2 * j + 1, 8, stride=nodes), :] = jnp.where(left8, swap(even), odd)
        return c

    lax.fori_loop(0, 32, lay, 0)
    for q in range(6):
        h, l = split2(wf[q * nodes : (q + 1) * nodes])
        whi[:, q * 128 : (q + 1) * 128] = h
        wlo[:, q * 128 : (q + 1) * 128] = l

    def three(a, b, bl, dot):
        h, l = split2(a)
        return dot(h, b) + (dot(l, b) + dot(h, bl))

    toward = three(lam[...], whi[...], wlo[...], nn)
    pack(ts, toward[:, 384:512], toward[:, 512:640], toward[:, 640:768])
    t_up = remote(ts.at[0], tr.at[1], 9, prev)
    t_down = remote(ts.at[1], tr.at[0], 8, nxt)

    def send_back(back, fwd):
        send(fwd, back)

    send_back(t_up, t_down)

    def flux_pair(i):
        to_prev = remote(hs.at[i, 0], hr.at[i, 1], 2 * (2 + i) + 1, prev)
        to_next = remote(hs.at[i, 1], hr.at[i, 0], 2 * (2 + i), nxt)
        return to_prev, to_next

    def send_flux(i):
        flux = three(gamb[...], whi[...], wlo[...], nn)
        pack(hs.at[i], flux[:, 384:512], flux[:, 512:640], flux[:, 640:768])
        to_prev, to_next = flux_pair(i)
        send(to_next, to_prev)
        qb[...] = -flux[:, 0:384]

    def neighbours(i, x):
        arrive(*pair(fs.at[i], fr.at[i], i))
        ext[:, 0:384] = x
        a, b, c = unpack(fr.at[i], ROWS)
        ext[:, 384:512] = a
        ext[:, 512:640] = b
        ext[:, 640:768] = c
        return three(ext[...], whi[...], wlo[...], nt)

    def flux_in(i):
        to_prev, to_next = flux_pair(i)
        arrive(to_next, to_prev)
        rows = ROWS
        left = left_mask(HALF)
        up, down = hr[i, 1, rows : rows + HALF], hr[i, 0, rows : rows + HALF]
        middle = jnp.concatenate(
            [jnp.where(left, up, swap(down)), jnp.where(left, swap(up), down)], axis=0
        )
        return jnp.concatenate([hr[i, 1, 0:rows], middle, hr[i, 0, 0:rows]], axis=1)

    def fold(x):
        x = x[:, 0:128] + x[:, 128:256] + x[:, 256:384]
        total = x[0:8]
        for i in range(1, ROWS // 8):
            total = total + x[8 * i : 8 * i + 8]
        return total

    def all_copy(i, off):
        peer = lax.rem(me + off, n)
        return pltpu.make_async_remote_copy(
            src_ref=allb.at[i, me], dst_ref=allb.at[i, me],
            send_sem=all_send.at[i], recv_sem=all_recv.at[i],
            device_id={"space": peer}, device_id_type=MESH,
        )

    def send_products(i, x, coupled, z):
        weight = wide(scale_ref[1])
        allb[i, me, 0:8] = fold(x * x * weight)
        allb[i, me, 8:16] = fold((x * coupled - 2.0 * gamb[...] * z) * weight)

        def go(off, c):
            all_copy(i, off).start()
            return c

        lax.fori_loop(1, n, go, 0)

    def products(i):
        others = allb.at[i, pl.ds(0, n - 1)]
        pltpu.make_async_copy(others, others, all_recv.at[i]).wait()
        pltpu.make_async_copy(others, others, all_send.at[i]).wait()
        total = allb[i, 0]
        for d in range(1, n):
            total = total + allb[i, d]
        return (
            jnp.sum(total[0:8], keepdims=True),
            jnp.sum(total[8:16], keepdims=True),
        )

    def couple_neighbours(z):
        h, l = split2(z)
        accb[...] = z

        def step(k, c):
            y = nn(coup_ref[k], h) + nn(coup_ref[k], l)
            accb[...] += lam[pl.ds(k, 1)] * y
            return c

        lax.fori_loop(0, VARS, step, 0)
        qb[...] -= accb[...]

    send_flux(0)
    z = neighbours(0, fieldb[...])
    ones = jnp.ones((16, 768), BF16)
    row_total = (nt(ones, whi[...]) + nt(ones, wlo[...]))[0:1]
    send_t = (t_down, t_up)
    arrive(*send_t)
    left = left_mask(8)
    up, down = tr[1, 16:24], tr[0, 16:24]
    middle = jnp.concatenate(
        [jnp.where(left, up, swap(down)), jnp.where(left, swap(up), down)], axis=0
    )
    came = jnp.concatenate([tr[1, 0:16], middle, tr[0, 0:16]], axis=1)
    dmode[...] = toward[:, 0:384] + came + row_total * lam[...]
    dmode[8:9] += cap
    cplb[...] = dmode[8:9] * fieldb[...]

    def join(k, c):
        cplb[...] += dmode[pl.ds(k, 1)] * ybuf[k]
        return c

    lax.fori_loop(0, VARS, join, 0)
    send_products(0, fieldb[...], cplb[...], z)
    couple_neighbours(z)
    image0 = qb[...] + cplb[...] - flux_in(0)
    norm0, product0 = products(0)
    step0 = norm0 / product0
    qb0 = image0
    r1b[...] = fieldb[...] - step0 * image0
    ext_q = ybuf
    send_field(1, r1b[...])

    h, l = split2(r1b[...])
    accb[...] = r1b[...]
    cplb[...] = dmode[8:9] * r1b[...]
    ext_q[0] = qb0

    def both(k, c):
        y = nn(coup_ref[k], h) + nn(coup_ref[k], l)
        accb[...] += lam[pl.ds(k, 1)] * y
        cplb[...] += dmode[pl.ds(k, 1)] * y
        return c

    lax.fori_loop(0, VARS, both, 0)
    gamb[...] = accb[...]
    send_flux(1)
    z = neighbours(1, r1b[...])
    send_products(1, r1b[...], cplb[...], z)
    couple_neighbours(z)
    norm1, product1 = products(1)
    ratio = norm1 / norm0
    step1 = norm1 / (product1 - ratio * norm1 / step0)

    def put_back(x):
        h, m, l = split3(x)
        y = nt(h, order) + (nt(m, order) + nt(l, order))
        return (y * wide(scale_ref[2]))[0:terms]

    x_ref[...] = put_back((step0 + step1 * ratio) * fieldb[...] + step1 * r1b[...])
    image1 = qb[...] + cplb[...] - flux_in(1)
    r_ref[...] = put_back(r1b[...] - step1 * (image1 + ratio * ext_q[0]))

    for i in range(2):
        sent(*pair(fs.at[i], fr.at[i], i))
        to_prev, to_next = flux_pair(i)
        sent(to_next, to_prev)
    sent(*send_t)


def shards(right_side, capacity, base_cond, var_field, block_cols, send_list):
    n = lax.axis_size("space")
    terms, nodes = right_side.shape
    blocks, slots, area = base_cond.shape
    width = nodes // blocks
    ups, downs = send_list[0, 0], send_list[0, 1]
    perm = jnp.concatenate([ups, downs[2:3], downs[0:2]])
    local = jnp.arange(blocks, dtype=jnp.int32)
    place = jnp.sum(
        jnp.where(perm[:, None] == local[None, :], local[:, None], 0), axis=0, dtype=jnp.int32
    )
    source = (perm[:, None] * width + jnp.arange(width, dtype=jnp.int32)[None, :]).reshape(1, nodes)
    columns = jnp.concatenate([local[:, None], block_cols], axis=1)
    inside = jnp.sum(
        jnp.where(columns[:, :, None] == local, place, 0), axis=2, dtype=jnp.int32
    )
    outside = jnp.where(columns < 9, columns, jnp.where(columns == 11, 9, columns + 1))
    where = jnp.where(columns < blocks, inside, outside)
    target = place[:, None] * 16 + (where % 2) * 8 + where // 2
    codes = jnp.concatenate([source, target.reshape(1, blocks * slots)], axis=1)
    codes = jnp.pad(codes, ((0, 0), (0, 640 - codes.shape[1])), constant_values=-1)
    coupling, scales = chaos_tables()
    vmem = pl.BlockSpec(memory_space=pltpu.VMEM)
    field = pltpu.VMEM((ROWS, nodes), F32)
    return pl.pallas_call(
        functools.partial(kernel, n),
        out_shape=(
            jax.ShapeDtypeStruct((terms, nodes), F32),
            jax.ShapeDtypeStruct((terms, nodes), F32),
        ),
        in_specs=[vmem] * 6 + [pl.BlockSpec(memory_space=pl.ANY)],
        out_specs=(vmem, vmem),
        scratch_shapes=[
            pltpu.VMEM((ROWS + 16, nodes), F32),
            pltpu.VMEM((blocks * slots, area), F32),
            pltpu.VMEM((blocks * 16, area), F32),
            pltpu.VMEM((8 * nodes, 128), F32),
            pltpu.VMEM((nodes, 2 * nodes), BF16),
            pltpu.VMEM((nodes, 2 * nodes), BF16),
            pltpu.VMEM((VARS, ROWS, nodes), F32),
            pltpu.VMEM((ROWS, 2 * nodes), F32),
            pltpu.VMEM((16, nodes), F32),
            pltpu.VMEM((16, nodes), F32),
            field, field, field, field, field, field,
            pltpu.VMEM((2, 2, MSG, 128), F32),
            pltpu.VMEM((2, 2, MSG, 128), F32),
            pltpu.VMEM((2, 2, MSG, 128), F32),
            pltpu.VMEM((2, 2, MSG, 128), F32),
            pltpu.VMEM((2, 24, 128), F32),
            pltpu.VMEM((2, 24, 128), F32),
            pltpu.VMEM((2, n, 16, 128), F32),
            pltpu.SemaphoreType.DMA((4,)),
            pltpu.SemaphoreType.DMA((10,)),
            pltpu.SemaphoreType.DMA((10,)),
            pltpu.SemaphoreType.DMA((2,)),
            pltpu.SemaphoreType.DMA((2,)),
        ],
        compiler_params=pltpu.CompilerParams(
            collective_id=0, has_side_effects=True, vmem_limit_bytes=48 * 1024 * 1024
        ),
        name="galerkin_cg",
    )(
        right_side, var_field, capacity.reshape(1, nodes), codes,
        jnp.asarray(coupling, BF16), jnp.asarray(scales), base_cond.reshape(blocks * slots, area),
    )


def solution(mesh):
    return jax.shard_map(
        shards,
        mesh=mesh,
        in_specs=(
            P(None, ("grp", "space")),
            P(("grp", "space")),
            P(("grp", "space"), None, None),
            P(None, ("grp", "space")),
            P(("grp", "space"), None),
            P(("grp", "space"), None, None),
        ),
        out_specs=(P(None, ("grp", "space")), P(None, ("grp", "space"))),
        check_vma=False,
    )
```

profile of v0, /device:TPU:0, one launch (start us, length us, event | category | flops | bytes accessed | tf_op | source)
XLA Modules:
  0.0 45.2 jit_solution(16299399991394400153)
XLA Ops:
  0.6 1.3 %slice.15 = s32[1,1,1]{2,1,0:T(1,128)} slice(s32[1,2,3]{2,1,0:T(2,128)} %param.13), slice={[0:1], [1:2], [2:3]} | slice | bytes 8 | tf_op jit(solution)/shard_map/slice | solution.py:419
  1.9 0.7 %slice_bitcast_fusion.1 = s32[3]{0:T(128)S(1)} fusion(s32[1,2,3]{2,1,0:T(2,128)} %param.13), kind=kLoop, calls=%fused_computation.20 | loop fusion | bytes 24 | tf_op jit(solution)/shard_map/concatenate | solution.py:419
  2.6 0.7 %slice_bitcast_fusion = s32[2]{0:T(128)S(1)} fusion(s32[1,2,3]{2,1,0:T(2,128)} %param.13), kind=kLoop, calls=%fused_computation.19 | loop fusion | bytes 16 | tf_op jit(solution)/shard_map/concatenate | solution.py:419
  3.3 0.7 %broadcast_multiply_fusion.1 = (s32[6]{0:T(128)S(1)}, s32[6]{0:T(128)S(1)}) fusion(s32[2]{0:T(128)S(1)} %slice_bitcast_fusion, s32[1]{0:T(128)} %bitcast.1, s32[3]{0:T(128)S(1)} %slice_bitcast_fusion.1), kind=kLoop, calls=%fused_computation.22 | loop fusion | flops 18 | bytes 72 | tf_op jit(solution)/shard_map/mul | solution.py:424
  4.0 0.1 select_reduce_fusion.1
  4.1 0.7 %reshape.209.cap_ref = f32[1,384]{1,0:T(1,128)S(1)} reshape(f32[384]{0:T(512)} %param.9) | data formatting | bytes 3072 | tf_op jit(solution)/shard_map/reshape | solution.py:475
  4.8 0.1 add.90
  4.8 0.1 add.91
  4.9 0.1 iota_add_fusion
  5.0 0.1 add.89
  5.1 0.8 %pad_add_fusion = s32[6,24]{1,0:T(8,128)S(1)} fusion(s32[6,23]{1,0:T(8,128)} %param.12, s32[6,1]{1,0:T(8,128)S(1)} %iota.16), kind=kLoop, calls=%fused_computation.3 | loop fusion | flops 144 | bytes 1152 | tf_op jit(solution)/shard_map/concatenate | solution.py:425
  5.8 0.1 concatenate.26
  5.9 0.1 select_reduce_fusion
  6.0 0.1 reduce_sum.22
  6.1 0.0 copy-start
  6.1 1.7 %copy-done = f32[6,24,4096]{2,1,0:T(8,128)S(1)} copy-done((f32[6,24,4096]{2,1,0:T(8,128)S(1)}, f32[6,24,4096]{2,1,0:T(8,128)}, u32[]{:S(2)}) %copy-start) | copy-done | bytes 2359320
  7.8 0.0 copy-start.1
  7.8 1.1 %copy-done.1 = bf16[8,176,176]{2,1,0:T(8,128)(2,1)S(1)} copy-done((bf16[8,176,176]{2,1,0:T(8,128)(2,1)S(1)}, bf16[8,176,176]{2,1,0:T(8,128)(2,1)}, u32[]{:S(2)}) %copy-start.1) | copy-done | bytes 495640
  8.9 1.0 %copy-done.2 = f32[3,176,128]{2,1,0:T(8,128)S(1)} copy-done((f32[3,176,128]{2,1,0:T(8,128)S(1)}, f32[3,176,128]{2,1,0:T(8,128)}, u32[]{:S(2)}) %copy-start.2) | copy-done | bytes 270360
  9.9 0.9 %copy-done.3 = f32[165,384]{1,0:T(8,128)S(1)} copy-done((f32[165,384]{1,0:T(8,128)S(1)}, f32[165,384]{1,0:T(8,128)}, u32[]{:S(2)}) %copy-start.3) | copy-done | bytes 253464
  10.8 0.7 %copy-done.4 = f32[8,384]{1,0:T(8,128)S(1)} copy-done((f32[8,384]{1,0:T(8,128)S(1)}, f32[8,384]{1,0:T(8,128)}, u32[]{:S(2)}) %copy-start.4) | copy-done | bytes 12312
  11.5 32.3 %galerkin_cg.1 = (f32[165,384]{1,0:T(8,128)S(1)}, f32[165,384]{1,0:T(8,128)S(1)}) custom-call(f32[165,384]{1,0:T(8,128)S(1)} %copy-done.3, f32[8,384]{1,0:T(8,128)S(1)} %copy-done.4, f32[1,384]{1,0:T(1,128)S(1)} %reshape.209.cap_ref, s32[1,640]{1,0:T(1,128)S(1)} %pad.4.codes_ref, bf16[8,176,176]{2,1,0:T(8,128)(2,1)S(1)} %copy-done.1, ...), custom_call_target="tpu_custom_call" | custom-call | tf_op jit(solution)/shard_map/galerkin_cg/pallas_call | solution.py:437
  43.8 0.7 %copy.12 = f32[165,384]{1,0:T(8,128)} copy(f32[165,384]{1,0:T(8,128)S(1)} %get-tuple-element.6) | data formatting | bytes 506880
  44.5 0.7 %copy.13 = f32[165,384]{1,0:T(8,128)} copy(f32[165,384]{1,0:T(8,128)S(1)} %get-tuple-element.7) | data formatting | bytes 506880
  (8 shorter events, 0.0 us)
Async XLA Ops:
  6.1 1.7 %copy-start = (f32[6,24,4096]{2,1,0:T(8,128)S(1)}, f32[6,24,4096]{2,1,0:T(8,128)}, u32[]{:S(2)}) copy-start(f32[6,24,4096]{2,1,0:T(8,128)} %param.10) | copy-start | bytes 7077892
  7.8 1.1 %copy-start.1 = (bf16[8,176,176]{2,1,0:T(8,128)(2,1)S(1)}, bf16[8,176,176]{2,1,0:T(8,128)(2,1)}, u32[]{:S(2)}) copy-start(bf16[8,176,176]{2,1,0:T(8,128)(2,1)} %constant.46.clone.coup_ref) | copy-start | bytes 1486852
  8.9 1.0 %copy-start.2 = (f32[3,176,128]{2,1,0:T(8,128)S(1)}, f32[3,176,128]{2,1,0:T(8,128)}, u32[]{:S(2)}) copy-start(f32[3,176,128]{2,1,0:T(8,128)} %constant.47.clone.scale_ref) | copy-start | bytes 811012
  9.9 0.9 %copy-start.3 = (f32[165,384]{1,0:T(8,128)S(1)}, f32[165,384]{1,0:T(8,128)}, u32[]{:S(2)}) copy-start(f32[165,384]{1,0:T(8,128)} %rhs_ref.1) | copy-start | bytes 760324
  10.8 0.7 %copy-start.4 = (f32[8,384]{1,0:T(8,128)S(1)}, f32[8,384]{1,0:T(8,128)}, u32[]{:S(2)}) copy-start(f32[8,384]{1,0:T(8,128)} %var_ref.1) | copy-start | bytes 36868
where the time goes:
time: 45.6 us; the launch traced here: 45.2 us
  Pallas kernels  32.3 us (71%)
  local copies, waits for them, and re-layouts  10.5 us (23%)
  other arithmetic  1.75 us (4%)
  between operations  0.68 us (1%)
    pallas_call x1, Pallas kernels, shards(): pl.pallas_call(functools.partial(kernel, n), out_shape=(jax.ShapeDtypeStr...  32.3 us
    unnamed x12, local copies, waits for them, and re-layouts  6.77 us
    concatenate x2, local copies, waits for them, and re-layouts, shards(): perm = jnp.concatenate([ups, downs[2:3], downs[0:2]])  1.36 us
    slice x1, local copies, waits for them, and re-layouts, shards(): perm = jnp.concatenate([ups, downs[2:3], downs[0:2]])  1.26 us

commit v1 on v0

v1 whole, which is shorter than its diff:
```python
import functools
import math

import jax
import jax.numpy as jnp
import numpy as np
from jax import lax
from jax.experimental import pallas as pl
from jax.experimental.pallas import tpu as pltpu
from jax.sharding import PartitionSpec as P

VARS = 8
ORDER = 3
ITERS = 2
SPREAD = 0.14
ROWS = 176
LOW, GAP, DEEP, LIVE = 45, 3, 48, 168
HALF = ROWS // 2
MSG = LIVE + HALF
MESH = pl.DeviceIdType.MESH
F32 = jnp.float32
BF16 = jnp.bfloat16


def chaos_tables():
    entries = []

    def grow(prefix, left):
        if len(prefix) == VARS:
            entries.append(tuple(prefix))
            return
        for degree in range(left + 1):
            grow(prefix + [degree], left - degree)

    grow([], ORDER)
    entries.sort(key=lambda m: (sum(m), tuple(-v for v in m)))
    lookup = {m: i if i < LOW else i + GAP for i, m in enumerate(entries)}
    coupling = np.zeros((768, 2 * ROWS), np.float32)
    expand = np.zeros((384, 16), np.float32)
    scale = np.ones((ROWS,), np.float64)
    for m, i in lookup.items():
        scale[i] = math.sqrt(math.prod(math.factorial(v) for v in m))
        held = [k for k in range(VARS) if m[k] > 0]
        for k in range(VARS):
            lowered = lookup.get(m[:k] + (m[k] - 1,) + m[k + 1 :])
            raised = lookup.get(m[:k] + (m[k] + 1,) + m[k + 1 :])
            for shift in (0, ROWS):
                if i < DEEP:
                    if lowered is not None:
                        coupling[DEEP * k + i, shift + lowered] = m[k]
                    coupling[DEEP * k + i, shift + raised] = 1.0
                elif m[k] > 0:
                    place = 120 * held.index(k) + i - DEEP
                    coupling[384 + place, shift + lowered] = m[k]
                    expand[place, k] = 1.0
    scales = np.stack([scale, 1.0 / scale**2, 1.0 / scale], 0)
    scales = np.broadcast_to(scales[:, :, None], (3, ROWS, 128)).astype(np.float32)
    return coupling, expand, scales


def split2(x):
    hi = x.astype(BF16)
    return hi, (x - hi.astype(F32)).astype(BF16)


def split3(x):
    hi = x.astype(BF16)
    rest = x - hi.astype(F32)
    mid = rest.astype(BF16)
    return hi, mid, (rest - mid.astype(F32)).astype(BF16)


def nn(a, b):
    return lax.dot_general(a, b, (((1,), (0,)), ((), ())), preferred_element_type=F32)


def nt(a, b):
    return lax.dot_general(a, b, (((1,), (1,)), ((), ())), preferred_element_type=F32)


def swap(x):
    return pltpu.roll(x, 64, 1)


def wide(x):
    return jnp.concatenate([x, x, x], axis=1)


def kernel(
    n,
    rhs_hbm, var_hbm, cap_hbm, cols_hbm, list_hbm, coup_hbm, expand_hbm, scale_hbm, base_hbm,
    x_ref, r_ref,
    rhs, var, capv, colv, lists, coup, expand, scale, base,
    inp, blk, wc, wf, whi, wlo, ybuf, xs, ext, lam, lamx, dmode, dmodex,
    fieldb, gamb, cplb, qb, r1b,
    fs, fr, hs, hr, ts, tr, allb,
    in_sem, base_sem, send_sem, recv_sem, all_send, all_recv,
):
    me = lax.axis_index("space")
    prev, nxt = lax.rem(me + n - 1, n), lax.rem(me + 1, n)
    chunk = base.shape[1] // 4

    ins = [
        pltpu.make_async_copy(src, dst, in_sem.at[i])
        for i, (src, dst) in enumerate(
            (
                (list_hbm, lists), (rhs_hbm, rhs), (var_hbm, var), (cap_hbm, capv),
                (cols_hbm, colv), (scale_hbm, scale), (coup_hbm, coup), (expand_hbm, expand),
            )
        )
    ]

    def base_copy(i):
        cols = pl.ds(i * chunk, chunk)
        return pltpu.make_async_copy(base_hbm.at[:, cols], base.at[:, cols], base_sem.at[i])

    for copy in ins:
        copy.start()
    for i in range(4):
        base_copy(i).start()

    barrier = pltpu.get_barrier_semaphore()

    def greet(i, c):
        pl.semaphore_signal(
            barrier, inc=1, device_id={"space": lax.rem(me + i, n)}, device_id_type=MESH
        )
        return c

    lax.fori_loop(1, n, greet, 0)

    def remote(src, dst, which, peer):
        return pltpu.make_async_remote_copy(
            src_ref=src, dst_ref=dst, send_sem=send_sem.at[which], recv_sem=recv_sem.at[which],
            device_id={"space": peer}, device_id_type=MESH,
        )

    def pair(src, dst, e):
        return remote(src.at[0], dst.at[0], 2 * e, nxt), remote(src.at[1], dst.at[1], 2 * e + 1, prev)

    def send(up, down):
        @pl.when(me < n - 1)
        def _():
            up.start()

        @pl.when(me > 0)
        def _():
            down.start()

    def arrive(up, down):
        @pl.when(me > 0)
        def _():
            up.wait_recv()

        @pl.when(me < n - 1)
        def _():
            down.wait_recv()

    def sent(up, down):
        @pl.when(me < n - 1)
        def _():
            up.wait_send()

        @pl.when(me > 0)
        def _():
            down.wait_send()

    def left_mask(rows):
        return lax.broadcasted_iota(jnp.int32, (rows, 128), 1) < 64

    def halves(left_of, right_of):
        return jnp.where(left_mask(left_of.shape[0]), left_of, right_of)

    def pack(first_dst, last_dst, first, middle, last):
        half = middle.shape[0] // 2
        rows = first_dst.shape[0] - half
        top, low = middle[:half], middle[half:]
        first_dst[0:rows] = first[:rows]
        first_dst[rows : rows + half] = halves(top, swap(low))
        last_dst[0:rows] = last[:rows]
        last_dst[rows : rows + half] = halves(swap(top), low)

    def unpack(first_src, last_src, half):
        rows = first_src.shape[0] - half
        a, b = first_src[rows : rows + half], last_src[rows : rows + half]
        middle = jnp.concatenate([halves(a, swap(b)), halves(swap(a), b)], axis=0)
        first, last = first_src[0:rows], last_src[0:rows]
        if rows < 2 * half:
            pad = jnp.zeros((2 * half - rows, 128), F32)
            first = jnp.concatenate([first, pad], axis=0)
            last = jnp.concatenate([last, pad], axis=0)
        return first, middle, last

    @pl.when(me == 0)
    def _():
        for buf in (fr.at[0, 0], fr.at[1, 0], hr.at[0, 0], hr.at[1, 0], tr.at[0]):
            buf[...] = jnp.zeros(buf.shape, F32)

    @pl.when(me == n - 1)
    def _():
        for buf in (fr.at[0, 1], fr.at[1, 1], hr.at[0, 1], hr.at[1, 1], tr.at[1]):
            buf[...] = jnp.zeros(buf.shape, F32)

    nodes = rhs.shape[1]
    terms = rhs.shape[0]
    inp[...] = jnp.zeros_like(inp)
    for copy in ins[:4]:
        copy.wait()
    perm = [lists[0, 0, 0], lists[0, 0, 1], lists[0, 0, 2], lists[0, 1, 2], lists[0, 1, 0], lists[0, 1, 1]]
    place = []
    for r in range(6):
        at = jnp.int32(0)
        for t in range(1, 6):
            at = jnp.where(perm[t] == r, jnp.int32(t), at)
        place.append(at)
    inp[0:LOW] = rhs[0:LOW]
    inp[DEEP:LIVE] = rhs[LOW:terms]
    inp[ROWS : ROWS + 8] = var[...]
    inp[ROWS + 8 : ROWS + 9] = capv[...].reshape(1, nodes)

    def reorder(tiles, index):
        rows = tiles[0].shape[0]
        for t in range(3):
            other = swap(tiles[t])
            blk[2 * t, 0:rows] = halves(tiles[t], other)
            blk[2 * t + 1, 0:rows] = halves(other, tiles[t])
        return [halves(blk[index[2 * t], 0:rows], blk[index[2 * t + 1], 0:rows]) for t in range(3)]

    moved = reorder([inp[:, t * 128 : (t + 1) * 128] for t in range(3)], perm)
    ins[5].wait()
    for t in range(3):
        cols = slice(t * 128, (t + 1) * 128)
        fieldb[:, cols] = moved[t][:ROWS] * scale[0]
        lam[0:8, cols] = moved[t][ROWS : ROWS + 8] * SPREAD
        dmode[0:16, cols] = moved[t][ROWS : ROWS + 16]
    lam[8:9] = jnp.ones((1, nodes), F32)
    lam[9:16] = jnp.zeros((7, nodes), F32)
    cap = dmode[8:9]

    pl.semaphore_wait(barrier, n - 1)

    def send_field(i, x):
        pack(fs.at[i, 0], fs.at[i, 1], x[:, 0:128], x[:, 128:256], x[:, 256:384])
        send(*pair(fs.at[i], fr.at[i], i))

    send_field(0, fieldb[...])

    def split_to(dst, x, cols=slice(None)):
        h, l = split2(x)
        dst[0:ROWS, cols] = h
        dst[ROWS : 2 * ROWS, cols] = l

    def spread(x):
        split_to(xs, x)
        ybuf[...] = nn(coup[...], xs[...])

    def joined(x, w, wx):
        top = w[8:9] * x[0:DEEP]
        for k in range(VARS):
            top = top + w[k : k + 1] * ybuf[DEEP * k : DEEP * (k + 1)]
        low = w[8:9] * x[DEEP:LIVE]
        for s in range(3):
            low = low + wx[120 * s : 120 * s + 120] * ybuf[384 + 120 * s : 504 + 120 * s]
        return jnp.concatenate([top, low, jnp.zeros((ROWS - LIVE, nodes), F32)], axis=0)

    def expanded(w):
        h, m, l = split3(w[...])
        e = expand[...]
        return nn(e, h) + (nn(e, m) + nn(e, l))

    ins[6].wait()
    ins[7].wait()
    lamx[...] = expanded(lam)
    spread(fieldb[...])
    gamb[...] = joined(fieldb[...], lam, lamx)

    rowsc, rowse = wc.shape[0], base.shape[0]
    ins[4].wait()
    slots = rowse // 6
    lane = lax.broadcasted_iota(jnp.int32, (1, rowse), 1)
    owner = jnp.zeros((1, rowse), jnp.int32)
    for j in range(1, 6):
        owner = owner + jnp.where(lane >= slots * j, 1, 0)
    slot = lane - slots * owner
    repeat = lax.broadcasted_iota(jnp.int32, (slots - 1, rowse), 0) == slot - 1
    given = nn(colv[...].astype(F32).astype(BF16), repeat.astype(F32).astype(BF16))
    given = jnp.where(lax.broadcasted_iota(jnp.int32, given.shape, 0) == owner, given, 0.0)
    column = jnp.sum(given, axis=0, keepdims=True).astype(jnp.int32)
    column = jnp.where(slot == 0, owner, column)
    where = jnp.where(column < 9, column, jnp.where(column == 11, 9, column + 1))
    row = jnp.zeros((1, rowse), jnp.int32)
    for j in range(6):
        where = jnp.where(column == j, place[j], where)
        row = jnp.where(owner == j, place[j], row)
    target = row * 16 + (where & 1) * 8 + (where >> 1)
    pick = (
        lax.broadcasted_iota(jnp.int32, (rowsc, rowse), 0) == target
    ).astype(F32).astype(BF16)
    for i in range(4):
        base_copy(i).wait()
        for j in range(2):
            cols = slice(i * chunk + j * 512, i * chunk + j * 512 + 512)
            h, l = split2(base[:, cols])
            wc[:, cols] = nn(pick, h) + nn(pick, l)

    def lay(j, c):
        cols = pl.ds(pl.multiple_of(j * 128, 128), 128)
        for t in range(6):
            even = wc[t * 16 : t * 16 + 8, cols]
            odd = wc[t * 16 + 8 : t * 16 + 16, cols]
            wf[pl.ds(t * 64 + 2 * j, 8, stride=nodes), :] = halves(even, swap(odd))
            wf[pl.ds(t * 64 + 2 * j + 1, 8, stride=nodes), :] = halves(swap(even), odd)
        return c

    lax.fori_loop(0, 32, lay, 0, unroll=4)
    for q in range(6):
        h, l = split2(wf[q * nodes : (q + 1) * nodes])
        whi[:, q * 128 : (q + 1) * 128] = h
        wlo[:, q * 128 : (q + 1) * 128] = l

    h, l = split2(lam[...])
    toward = nn(h, whi[...]) + (nn(l, whi[...]) + nn(h, wlo[...]))
    pack(ts.at[0], ts.at[1], toward[:, 384:512], toward[:, 512:640], toward[:, 640:768])
    t_pair = (remote(ts.at[1], tr.at[0], 8, nxt), remote(ts.at[0], tr.at[1], 9, prev))
    send(*t_pair)

    def edges(src, dot):
        both = dot(src[...], whi[...])
        return both[0:ROWS] + both[ROWS : 2 * ROWS] + dot(src[0:ROWS], wlo[...])

    def flux_pair(i):
        to_prev = remote(hs.at[i, 0], hr.at[i, 1], 2 * (2 + i) + 1, prev)
        to_next = remote(hs.at[i, 1], hr.at[i, 0], 2 * (2 + i), nxt)
        return to_next, to_prev

    def send_flux(i):
        split_to(xs, gamb[...])
        flux = edges(xs, nn)
        pack(hs.at[i, 0], hs.at[i, 1], flux[:, 384:512], flux[:, 512:640], flux[:, 640:768])
        send(*flux_pair(i))
        qb[...] = -flux[:, 0:384]

    def neighbours(i, x):
        split_to(ext, x, slice(0, 384))
        arrive(*pair(fs.at[i], fr.at[i], i))
        for t, tile in enumerate(unpack(fr.at[i, 0], fr.at[i, 1], HALF)):
            split_to(ext, tile, slice(384 + t * 128, 512 + t * 128))
        return edges(ext, nt)

    def flux_in(i):
        arrive(*flux_pair(i))
        return jnp.concatenate(unpack(hr.at[i, 1], hr.at[i, 0], HALF), axis=1)

    def fold(x):
        x = x[:, 0:128] + x[:, 128:256] + x[:, 256:384]
        total = x[0:8]
        for i in range(1, ROWS // 8):
            total = total + x[8 * i : 8 * i + 8]
        return total

    def all_copy(i, off):
        return pltpu.make_async_remote_copy(
            src_ref=allb.at[i, me], dst_ref=allb.at[i, me],
            send_sem=all_send.at[i], recv_sem=all_recv.at[i],
            device_id={"space": lax.rem(me + off, n)}, device_id_type=MESH,
        )

    def send_products(i, x, coupled, z):
        weight = wide(scale[1])
        allb[i, me, 0:8] = fold(x * x * weight)
        allb[i, me, 8:16] = fold((x * coupled - 2.0 * gamb[...] * z) * weight)

        def go(off, c):
            all_copy(i, off).start()
            return c

        lax.fori_loop(1, n, go, 0)

    def products(i):
        others = allb.at[i, pl.ds(0, n - 1)]
        pltpu.make_async_copy(others, others, all_recv.at[i]).wait()
        pltpu.make_async_copy(others, others, all_send.at[i]).wait()
        total = allb[i, 0]
        for d in range(1, n):
            total = total + allb[i, d]
        return jnp.sum(total[0:8], keepdims=True), jnp.sum(total[8:16], keepdims=True)

    def couple_neighbours(z):
        spread(z)
        qb[...] += cplb[...] - joined(z, lam, lamx)

    send_flux(0)
    ones = jnp.ones((16, 768), BF16)
    row_total = (nt(ones, whi[...]) + nt(ones, wlo[...]))[0:1]
    arrive(*t_pair)
    came = jnp.concatenate(unpack(tr.at[1], tr.at[0], 8), axis=1)
    dmode[...] = toward[:, 0:384] + came + row_total * lam[...] + jnp.where(
        lax.broadcasted_iota(jnp.int32, (16, nodes), 0) == 8, cap, 0.0
    )
    dmodex[...] = expanded(dmode)
    cplb[...] = joined(fieldb[...], dmode, dmodex)
    z = neighbours(0, fieldb[...])
    send_products(0, fieldb[...], cplb[...], z)
    couple_neighbours(z)
    image0 = qb[...] - flux_in(0)
    norm0, product0 = products(0)
    step0 = norm0 / product0
    r1b[...] = fieldb[...] - step0 * image0
    send_field(1, r1b[...])

    spread(r1b[...])
    gamb[...] = joined(r1b[...], lam, lamx)
    send_flux(1)
    cplb[...] = joined(r1b[...], dmode, dmodex)
    z = neighbours(1, r1b[...])
    send_products(1, r1b[...], cplb[...], z)
    couple_neighbours(z)

    def put_back(x):
        tiles = reorder([x[:, t * 128 : (t + 1) * 128] for t in range(3)], place)
        return jnp.concatenate([tile * scale[2] for tile in tiles], axis=1)

    def put_out(ref, y):
        ref[0:LOW] = y[0:LOW]
        ref[LOW:terms] = y[DEEP:LIVE]

    fieldb[...] = put_back(r1b[...])
    norm1, product1 = products(1)
    ratio = norm1 / norm0
    step1 = norm1 / (product1 - ratio * norm1 / step0)
    put_out(x_ref, (step0 + step1 * ratio) * inp[0:ROWS] + step1 * fieldb[...])
    gamb[...] = fieldb[...] - (step1 * ratio / step0) * (inp[0:ROWS] - fieldb[...])
    image1 = qb[...] - flux_in(1)
    put_out(r_ref, gamb[...] - step1 * put_back(image1))

    for i in range(2):
        sent(*pair(fs.at[i], fr.at[i], i))
        sent(*flux_pair(i))
    sent(*t_pair)


def shards(right_side, capacity, base_cond, var_field, block_cols, send_list):
    n = lax.axis_size("space")
    terms, nodes = right_side.shape
    blocks, slots, area = base_cond.shape
    coupling, expand, scales = chaos_tables()
    vmem = pl.BlockSpec(memory_space=pltpu.VMEM)
    field = pltpu.VMEM((ROWS, nodes), F32)
    small = pltpu.VMEM((16, nodes), F32)
    message = pltpu.VMEM((2, 2, MSG, 128), F32)
    return pl.pallas_call(
        functools.partial(kernel, n),
        out_shape=(
            jax.ShapeDtypeStruct((terms, nodes), F32),
            jax.ShapeDtypeStruct((terms, nodes), F32),
        ),
        in_specs=[pl.BlockSpec(memory_space=pl.ANY)] * 9,
        out_specs=(vmem, vmem),
        scratch_shapes=[
            pltpu.VMEM((terms, nodes), F32),
            pltpu.VMEM(var_field.shape, F32),
            pltpu.VMEM(capacity.shape, F32),
            pltpu.VMEM(block_cols.shape, jnp.int32),
            pltpu.SMEM(send_list.shape, jnp.int32),
            pltpu.VMEM(coupling.shape, BF16),
            pltpu.VMEM(expand.shape, BF16),
            pltpu.VMEM(scales.shape, F32),
            pltpu.VMEM((blocks * slots, area), F32),
            pltpu.VMEM((ROWS + 16, nodes), F32),
            pltpu.VMEM((blocks, ROWS + 16, 128), F32),
            pltpu.VMEM((blocks * 16, area), F32),
            pltpu.VMEM((8 * nodes, 128), F32),
            pltpu.VMEM((nodes, 2 * nodes), BF16),
            pltpu.VMEM((nodes, 2 * nodes), BF16),
            pltpu.VMEM((768, nodes), F32),
            pltpu.VMEM((2 * ROWS, nodes), BF16),
            pltpu.VMEM((2 * ROWS, 2 * nodes), BF16),
            small, pltpu.VMEM((384, nodes), F32), small, pltpu.VMEM((384, nodes), F32),
            field, field, field, field, field,
            message, message, message, message,
            pltpu.VMEM((2, 24, 128), F32),
            pltpu.VMEM((2, 24, 128), F32),
            pltpu.VMEM((2, n, 16, 128), F32),
            pltpu.SemaphoreType.DMA((8,)),
            pltpu.SemaphoreType.DMA((4,)),
            pltpu.SemaphoreType.DMA((10,)),
            pltpu.SemaphoreType.DMA((10,)),
            pltpu.SemaphoreType.DMA((2,)),
            pltpu.SemaphoreType.DMA((2,)),
        ],
        compiler_params=pltpu.CompilerParams(
            collective_id=0, has_side_effects=True, vmem_limit_bytes=60 * 1024 * 1024
        ),
        name="galerkin_cg",
    )(
        right_side, var_field, capacity, block_cols, send_list,
        jnp.asarray(coupling, BF16), jnp.asarray(expand, BF16), jnp.asarray(scales),
        base_cond.reshape(blocks * slots, area),
    )


def solution(mesh):
    return jax.shard_map(
        shards,
        mesh=mesh,
        in_specs=(
            P(None, ("grp", "space")),
            P(("grp", "space")),
            P(("grp", "space"), None, None),
            P(None, ("grp", "space")),
            P(("grp", "space"), None),
            P(("grp", "space"), None, None),
        ),
        out_specs=(P(None, ("grp", "space")), P(None, ("grp", "space"))),
        check_vma=False,
    )
```

time: 45.6 us -> 35.1 us (0.77)
  local copies, waits for them, and re-layouts: 10.5 us -> 3.32 us
  other arithmetic: 1.75 us -> 0 us
  Pallas kernels: 32.3 us -> 30.9 us
    unnamed x12 -> x2, local copies, waits for them, and re-layouts: 6.77 us -> 3.32 us
    concatenate x3 -> x0, local copies, waits for them, and re-layouts: 1.44 us -> none  [the longest x2 1.36 us: shards(): perm = jnp.concatenate([ups, downs[2:3], downs[0:2]])]
    pallas_call x1, Pallas kernels: 32.3 us -> 30.9 us  [shards(): pl.pallas_call(functools.partial(kernel, n), out_shape=(jax.ShapeDtypeStr...]
    slice x1 -> x0, local copies, waits for them, and re-layouts: 1.26 us -> none  [shards(): perm = jnp.concatenate([ups, downs[2:3], downs[0:2]])]
    concatenate x2 -> x0, other arithmetic: 0.77 us -> none  [the longest x1 0.76 us: shards(): columns = jnp.concatenate([local[:, None], block_cols], axis=1)]
    mul x2 -> x0, other arithmetic: 0.73 us -> none  [the longest x1 0.72 us: shards(): perm[:, None] * width + jnp.arange(width, dtype=jnp.int32)[None, :]]
    reshape x1 -> x0, local copies, waits for them, and re-layouts: 0.68 us -> none  [shards(): capacity.reshape(1, nodes)]
where the time goes in v1:
time: 35.1 us; the launch traced here: 34.9 us
  Pallas kernels  30.9 us (88%)
  local copies, waits for them, and re-layouts  3.32 us (9%)
  between operations  0.64 us (2%)
    pallas_call x1, Pallas kernels, shards(): pl.pallas_call(functools.partial(kernel, n), out_shape=(jax.ShapeDtypeStr...  30.9 us
    unnamed x2, local copies, waits for them, and re-layouts  3.32 us

profile of v1, /device:TPU:0, one launch (start us, length us, event | category | flops | bytes accessed | tf_op | source)
XLA Modules:
  0.0 34.9 jit_solution(10139693562740961355)
XLA Ops:
  0.6 30.9 %galerkin_cg.1 = (f32[165,384]{1,0:T(8,128)}, f32[165,384]{1,0:T(8,128)}) custom-call(f32[165,384]{1,0:T(8,128)} %rhs_hbm.1, f32[8,384]{1,0:T(8,128)} %var_hbm.1, f32[384]{0:T(512)} %cap_hbm.1, s32[6,23]{1,0:T(8,128)} %cols_hbm.1, s32[1,2,3]{2,1,0:T(2,128)} %list_hbm.1, bf16[768,352]{1,0:T(8,128)(2,1)} %constant.6.clone.coup_hbm, ...), custom_call_target="tpu_custom_call" | custom-call | tf_op jit(solution)/shard_map/galerkin_cg/pallas_call | solution.py:451
  31.6 1.7 %copy.13 = f32[165,384]{1,0:T(8,128)} copy(f32[165,384]{1,0:T(8,128)} %get-tuple-element.4) | data formatting | bytes 506880
  33.2 1.7 %copy.14 = f32[165,384]{1,0:T(8,128)} copy(f32[165,384]{1,0:T(8,128)} %get-tuple-element.5) | data formatting | bytes 506880

commit v2 on v1

--- a/solution.py
+++ b/solution.py
@@ -91,8 +91,8 @@
     rhs_hbm, var_hbm, cap_hbm, cols_hbm, list_hbm, coup_hbm, expand_hbm, scale_hbm, base_hbm,
     x_ref, r_ref,
     rhs, var, capv, colv, lists, coup, expand, scale, base,
-    inp, blk, wc, wf, whi, wlo, ybuf, xs, ext, lam, lamx, dmode, dmodex,
-    fieldb, gamb, cplb, qb, r1b,
+    inp, blk, wc, wf, whi, wlo, ybuf, xs, ext, lam, lamx, dmode, dmodex, caps,
+    fieldb, gamb, cplb, zb, imageb, gamq, cplq, qb, r1b,
     fs, fr, hs, hr, ts, tr, allb,
     in_sem, base_sem, send_sem, recv_sem, all_send, all_recv,
 ):
@@ -232,10 +232,10 @@
         cols = slice(t * 128, (t + 1) * 128)
         fieldb[:, cols] = moved[t][:ROWS] * scale[0]
         lam[0:8, cols] = moved[t][ROWS : ROWS + 8] * SPREAD
-        dmode[0:16, cols] = moved[t][ROWS : ROWS + 16]
+        caps[0:8, cols] = moved[t][ROWS + 8 : ROWS + 16]
     lam[8:9] = jnp.ones((1, nodes), F32)
     lam[9:16] = jnp.zeros((7, nodes), F32)
-    cap = dmode[8:9]
+    cap = caps[0:1]
 
     pl.semaphore_wait(barrier, n - 1)
 
@@ -252,7 +252,7 @@
 
     def spread(x):
         split_to(xs, x)
-        ybuf[...] = nn(coup[...], xs[...])
+        ybuf[...] = nn(coup[...], xs[0 : 2 * ROWS])
 
     def joined(x, w, wx):
         top = w[8:9] * x[0:DEEP]
@@ -308,24 +308,20 @@
         for t in range(6):
             even = wc[t * 16 : t * 16 + 8, cols]
             odd = wc[t * 16 + 8 : t * 16 + 16, cols]
-            wf[pl.ds(t * 64 + 2 * j, 8, stride=nodes), :] = halves(even, swap(odd))
-            wf[pl.ds(t * 64 + 2 * j + 1, 8, stride=nodes), :] = halves(swap(even), odd)
+            wf[pl.ds(t * 64 + 2 * j, 8, stride=nodes + 1), :] = halves(even, swap(odd))
+            wf[pl.ds(t * 64 + 2 * j + 1, 8, stride=nodes + 1), :] = halves(swap(even), odd)
         return c
 
     lax.fori_loop(0, 32, lay, 0, unroll=4)
     for q in range(6):
-        h, l = split2(wf[q * nodes : (q + 1) * nodes])
+        h, l = split2(wf[q * (nodes + 1) : q * (nodes + 1) + nodes])
         whi[:, q * 128 : (q + 1) * 128] = h
         wlo[:, q * 128 : (q + 1) * 128] = l
 
-    h, l = split2(lam[...])
-    toward = nn(h, whi[...]) + (nn(l, whi[...]) + nn(h, wlo[...]))
-    pack(ts.at[0], ts.at[1], toward[:, 384:512], toward[:, 512:640], toward[:, 640:768])
     t_pair = (remote(ts.at[1], tr.at[0], 8, nxt), remote(ts.at[0], tr.at[1], 9, prev))
-    send(*t_pair)
 
     def edges(src, dot):
-        both = dot(src[...], whi[...])
+        both = dot(src[0 : 2 * ROWS], whi[...])
         return both[0:ROWS] + both[ROWS : 2 * ROWS] + dot(src[0:ROWS], wlo[...])
 
     def flux_pair(i):
@@ -333,9 +329,22 @@
         to_next = remote(hs.at[i, 1], hr.at[i, 0], 2 * (2 + i), nxt)
         return to_next, to_prev
 
-    def send_flux(i):
-        split_to(xs, gamb[...])
-        flux = edges(xs, nn)
+    def send_flux(i, gam):
+        split_to(xs, gam[...])
+        if i == 0:
+            h, l = split2(lam[...])
+            xs[2 * ROWS : 2 * ROWS + 16] = h
+            xs[2 * ROWS + 16 : 2 * ROWS + 32] = l
+            fine = nn(xs[...], whi[...])
+            rest = jnp.concatenate([xs[0:ROWS], xs[2 * ROWS : 2 * ROWS + 16]], axis=0)
+            rest = nn(rest, wlo[...])
+            flux = fine[0:ROWS] + fine[ROWS : 2 * ROWS] + rest[0:ROWS]
+            toward = fine[2 * ROWS : 2 * ROWS + 16] + fine[2 * ROWS + 16 :] + rest[ROWS:]
+            pack(ts.at[0], ts.at[1], toward[:, 384:512], toward[:, 512:640], toward[:, 640:768])
+            send(*t_pair)
+            dmode[...] = toward[:, 0:384]
+        else:
+            flux = edges(xs, nn)
         pack(hs.at[i, 0], hs.at[i, 1], flux[:, 384:512], flux[:, 512:640], flux[:, 640:768])
         send(*flux_pair(i))
         qb[...] = -flux[:, 0:384]
@@ -365,10 +374,11 @@
             device_id={"space": lax.rem(me + off, n)}, device_id_type=MESH,
         )
 
-    def send_products(i, x, coupled, z):
+    def send_products(i, x, coupled, gam, z):
         weight = wide(scale[1])
-        allb[i, me, 0:8] = fold(x * x * weight)
-        allb[i, me, 8:16] = fold((x * coupled - 2.0 * gamb[...] * z) * weight)
+        norm = jnp.sum(fold(x * x * weight), axis=0, keepdims=True)
+        product = jnp.sum(fold((x * coupled - 2.0 * gam * z) * weight), axis=0, keepdims=True)
+        allb[i, me] = halves(norm + swap(norm), product + swap(product))
 
         def go(off, c):
             all_copy(i, off).start()
@@ -383,38 +393,45 @@
         total = allb[i, 0]
         for d in range(1, n):
             total = total + allb[i, d]
-        return jnp.sum(total[0:8], keepdims=True), jnp.sum(total[8:16], keepdims=True)
-
-    def couple_neighbours(z):
+        left = left_mask(1)
+        return (
+            jnp.sum(jnp.where(left, total, 0.0), keepdims=True),
+            jnp.sum(jnp.where(left, 0.0, total), keepdims=True),
+        )
+
+    def couple_neighbours(z, coupled):
         spread(z)
-        qb[...] += cplb[...] - joined(z, lam, lamx)
-
-    send_flux(0)
+        qb[...] += coupled - joined(z, lam, lamx)
+
+    send_flux(0, gamb)
     ones = jnp.ones((16, 768), BF16)
     row_total = (nt(ones, whi[...]) + nt(ones, wlo[...]))[0:1]
     arrive(*t_pair)
     came = jnp.concatenate(unpack(tr.at[1], tr.at[0], 8), axis=1)
-    dmode[...] = toward[:, 0:384] + came + row_total * lam[...] + jnp.where(
+    dmode[...] += came + row_total * lam[...] + jnp.where(
         lax.broadcasted_iota(jnp.int32, (16, nodes), 0) == 8, cap, 0.0
     )
     dmodex[...] = expanded(dmode)
     cplb[...] = joined(fieldb[...], dmode, dmodex)
-    z = neighbours(0, fieldb[...])
-    send_products(0, fieldb[...], cplb[...], z)
-    couple_neighbours(z)
-    image0 = qb[...] - flux_in(0)
+    zb[...] = neighbours(0, fieldb[...])
+    send_products(0, fieldb[...], cplb[...], gamb[...], zb[...])
+    couple_neighbours(zb[...], cplb[...])
+    imageb[...] = qb[...] - flux_in(0)
+    send_field(1, imageb[...])
+
+    spread(imageb[...])
+    gamq[...] = joined(imageb[...], lam, lamx)
+    cplq[...] = joined(imageb[...], dmode, dmodex)
+    send_flux(1, gamq)
+    z = neighbours(1, imageb[...])
     norm0, product0 = products(0)
     step0 = norm0 / product0
-    r1b[...] = fieldb[...] - step0 * image0
-    send_field(1, r1b[...])
-
-    spread(r1b[...])
-    gamb[...] = joined(r1b[...], lam, lamx)
-    send_flux(1)
-    cplb[...] = joined(r1b[...], dmode, dmodex)
-    z = neighbours(1, r1b[...])
-    send_products(1, r1b[...], cplb[...], z)
-    couple_neighbours(z)
+    r1b[...] = fieldb[...] - step0 * imageb[...]
+    send_products(
+        1, r1b[...], cplb[...] - step0 * cplq[...], gamb[...] - step0 * gamq[...],
+        zb[...] - step0 * z,
+    )
+    couple_neighbours(z, cplq[...])
 
     def put_back(x):
         tiles = reorder([x[:, t * 128 : (t + 1) * 128] for t in range(3)], place)
@@ -429,9 +446,9 @@
     ratio = norm1 / norm0
     step1 = norm1 / (product1 - ratio * norm1 / step0)
     put_out(x_ref, (step0 + step1 * ratio) * inp[0:ROWS] + step1 * fieldb[...])
-    gamb[...] = fieldb[...] - (step1 * ratio / step0) * (inp[0:ROWS] - fieldb[...])
-    image1 = qb[...] - flux_in(1)
-    put_out(r_ref, gamb[...] - step1 * put_back(image1))
+    gamb[...] = fieldb[...] - (step1 * (1.0 + ratio) / step0) * (inp[0:ROWS] - fieldb[...])
+    second = qb[...] - flux_in(1)
+    put_out(r_ref, gamb[...] + (step1 * step0) * put_back(second))
 
     for i in range(2):
         sent(*pair(fs.at[i], fr.at[i], i))
@@ -451,10 +468,10 @@
     return pl.pallas_call(
         functools.partial(kernel, n),
         out_shape=(
-            jax.ShapeDtypeStruct((terms, nodes), F32),
-            jax.ShapeDtypeStruct((terms, nodes), F32),
+            pltpu.VMEM((terms, nodes), F32),
+            pltpu.VMEM((terms, nodes), F32),
         ),
-        in_specs=[pl.BlockSpec(memory_space=pl.ANY)] * 9,
+        in_specs=[pl.BlockSpec(memory_space=pltpu.HBM)] * 9,
         out_specs=(vmem, vmem),
         scratch_shapes=[
             pltpu.VMEM((terms, nodes), F32),
@@ -469,18 +486,18 @@
             pltpu.VMEM((ROWS + 16, nodes), F32),
             pltpu.VMEM((blocks, ROWS + 16, 128), F32),
             pltpu.VMEM((blocks * 16, area), F32),
-            pltpu.VMEM((8 * nodes, 128), F32),
+            pltpu.VMEM((8 * nodes + 8, 128), F32),
             pltpu.VMEM((nodes, 2 * nodes), BF16),
             pltpu.VMEM((nodes, 2 * nodes), BF16),
             pltpu.VMEM((768, nodes), F32),
-            pltpu.VMEM((2 * ROWS, nodes), BF16),
+            pltpu.VMEM((2 * ROWS + 32, nodes), BF16),
             pltpu.VMEM((2 * ROWS, 2 * nodes), BF16),
-            small, pltpu.VMEM((384, nodes), F32), small, pltpu.VMEM((384, nodes), F32),
-            field, field, field, field, field,
+            small, pltpu.VMEM((384, nodes), F32), small, pltpu.VMEM((384, nodes), F32), small,
+            field, field, field, field, field, field, field, field, field,
             message, message, message, message,
             pltpu.VMEM((2, 24, 128), F32),
             pltpu.VMEM((2, 24, 128), F32),
-            pltpu.VMEM((2, n, 16, 128), F32),
+            pltpu.VMEM((2, n, 1, 128), F32),
             pltpu.SemaphoreType.DMA((8,)),
             pltpu.SemaphoreType.DMA((4,)),
             pltpu.SemaphoreType.DMA((10,)),

time: 35.1 us -> 28.4 us (0.81)
  Pallas kernels: 30.9 us -> 26.2 us
  local copies, waits for them, and re-layouts: 3.32 us -> 1.4 us
    pallas_call x1, Pallas kernels: 30.9 us -> 26.2 us  [shards(): pl.pallas_call(functools.partial(kernel, n), out_shape=(pltpu.VMEM((terms...]
    unnamed x2, local copies, waits for them, and re-layouts: 3.32 us -> 1.4 us
where the time goes in v2:
time: 28.4 us; the launch traced here: 28.2 us
  Pallas kernels  26.2 us (92%)
  local copies, waits for them, and re-layouts  1.4 us (5%)
  between operations  0.64 us (2%)
    pallas_call x1, Pallas kernels, shards(): pl.pallas_call(functools.partial(kernel, n), out_shape=(pltpu.VMEM((terms...  26.2 us
    unnamed x2, local copies, waits for them, and re-layouts  1.4 us

profile of v2, /device:TPU:0, one launch (start us, length us, event | category | flops | bytes accessed | tf_op | source)
XLA Modules:
  0.0 28.2 jit_solution(18109172937973656610)
XLA Ops:
  0.6 26.2 %galerkin_cg.1 = (f32[165,384]{1,0:T(8,128)S(1)}, f32[165,384]{1,0:T(8,128)S(1)}) custom-call(f32[165,384]{1,0:T(8,128)} %rhs_hbm.1, f32[8,384]{1,0:T(8,128)} %var_hbm.1, f32[384]{0:T(512)} %cap_hbm.1, s32[6,23]{1,0:T(8,128)} %cols_hbm.1, s32[1,2,3]{2,1,0:T(2,128)} %list_hbm.1, bf16[768,352]{1,0:T(8,128)(2,1)} %constant.6.clone.coup_hbm, ...), custom_call_target="tpu_custom_call" | custom-call | tf_op jit(solution)/shard_map/galerkin_cg/pallas_call | solution.py:468
  26.8 0.7 %copy.13 = f32[165,384]{1,0:T(8,128)} copy(f32[165,384]{1,0:T(8,128)S(1)} %get-tuple-element.2) | data formatting | bytes 506880
  27.6 0.7 %copy.14 = f32[165,384]{1,0:T(8,128)} copy(f32[165,384]{1,0:T(8,128)S(1)} %get-tuple-element.3) | data formatting | bytes 506880

commit v3 on v2

--- a/solution.py
+++ b/solution.py
@@ -17,6 +17,7 @@
 LOW, GAP, DEEP, LIVE = 45, 3, 48, 168
 HALF = ROWS // 2
 MSG = LIVE + HALF
+OWN, AWAY = slice(0, 384), slice(384, 768)
 MESH = pl.DeviceIdType.MESH
 F32 = jnp.float32
 BF16 = jnp.bfloat16
@@ -92,7 +93,7 @@
     x_ref, r_ref,
     rhs, var, capv, colv, lists, coup, expand, scale, base,
     inp, blk, wc, wf, whi, wlo, ybuf, xs, ext, lam, lamx, dmode, dmodex, caps,
-    fieldb, gamb, cplb, zb, imageb, gamq, cplq, qb, r1b,
+    fieldb, gamb, cplb, backb, imageb, cplq, backq, r1b,
     fs, fr, hs, hr, ts, tr, allb,
     in_sem, base_sem, send_sem, recv_sem, all_send, all_recv,
 ):
@@ -251,8 +252,7 @@
         dst[ROWS : 2 * ROWS, cols] = l
 
     def spread(x):
-        split_to(xs, x)
-        ybuf[...] = nn(coup[...], xs[0 : 2 * ROWS])
+        ybuf[...] = nn(coup[...], x)
 
     def joined(x, w, wx):
         top = w[8:9] * x[0:DEEP]
@@ -271,7 +271,8 @@
     ins[6].wait()
     ins[7].wait()
     lamx[...] = expanded(lam)
-    spread(fieldb[...])
+    split_to(ext, fieldb[...], OWN)
+    spread(ext[:, OWN])
     gamb[...] = joined(fieldb[...], lam, lamx)
 
     rowsc, rowse = wc.shape[0], base.shape[0]
@@ -313,59 +314,53 @@
         return c
 
     lax.fori_loop(0, 32, lay, 0, unroll=4)
-    for q in range(6):
+    for q in (3, 4, 5, 0, 1, 2):
         h, l = split2(wf[q * (nodes + 1) : q * (nodes + 1) + nodes])
         whi[:, q * 128 : (q + 1) * 128] = h
         wlo[:, q * 128 : (q + 1) * 128] = l
 
     t_pair = (remote(ts.at[1], tr.at[0], 8, nxt), remote(ts.at[0], tr.at[1], 9, prev))
 
-    def edges(src, dot):
-        both = dot(src[0 : 2 * ROWS], whi[...])
-        return both[0:ROWS] + both[ROWS : 2 * ROWS] + dot(src[0:ROWS], wlo[...])
+    def edges(src, cols, dot):
+        left = src[0 : 2 * ROWS, cols] if dot is nt else src[0 : 2 * ROWS]
+        both = dot(left, whi[:, cols])
+        return both[0:ROWS] + both[ROWS : 2 * ROWS] + dot(left[0:ROWS], wlo[:, cols])
 
     def flux_pair(i):
         to_prev = remote(hs.at[i, 0], hr.at[i, 1], 2 * (2 + i) + 1, prev)
         to_next = remote(hs.at[i, 1], hr.at[i, 0], 2 * (2 + i), nxt)
         return to_next, to_prev
 
-    def send_flux(i, gam):
-        split_to(xs, gam[...])
-        if i == 0:
-            h, l = split2(lam[...])
-            xs[2 * ROWS : 2 * ROWS + 16] = h
-            xs[2 * ROWS + 16 : 2 * ROWS + 32] = l
-            fine = nn(xs[...], whi[...])
-            rest = jnp.concatenate([xs[0:ROWS], xs[2 * ROWS : 2 * ROWS + 16]], axis=0)
-            rest = nn(rest, wlo[...])
-            flux = fine[0:ROWS] + fine[ROWS : 2 * ROWS] + rest[0:ROWS]
-            toward = fine[2 * ROWS : 2 * ROWS + 16] + fine[2 * ROWS + 16 :] + rest[ROWS:]
-            pack(ts.at[0], ts.at[1], toward[:, 384:512], toward[:, 512:640], toward[:, 640:768])
-            send(*t_pair)
-            dmode[...] = toward[:, 0:384]
-        else:
-            flux = edges(xs, nn)
-        pack(hs.at[i, 0], hs.at[i, 1], flux[:, 384:512], flux[:, 512:640], flux[:, 640:768])
+    def flux_and_weights(cols):
+        fine = nn(xs[...], whi[:, cols])
+        rest = jnp.concatenate([xs[0:ROWS], xs[2 * ROWS : 2 * ROWS + 16]], axis=0)
+        rest = nn(rest, wlo[:, cols])
+        return (
+            fine[0:ROWS] + fine[ROWS : 2 * ROWS] + rest[0:ROWS],
+            fine[2 * ROWS : 2 * ROWS + 16] + fine[2 * ROWS + 16 :] + rest[ROWS:],
+        )
+
+    def send_flux(i, flux):
+        pack(hs.at[i, 0], hs.at[i, 1], flux[:, 0:128], flux[:, 128:256], flux[:, 256:384])
         send(*flux_pair(i))
-        qb[...] = -flux[:, 0:384]
-
-    def neighbours(i, x):
-        split_to(ext, x, slice(0, 384))
-        arrive(*pair(fs.at[i], fr.at[i], i))
+
+    def outer(i):
         for t, tile in enumerate(unpack(fr.at[i, 0], fr.at[i, 1], HALF)):
             split_to(ext, tile, slice(384 + t * 128, 512 + t * 128))
-        return edges(ext, nt)
+        return edges(ext, AWAY, nt)
 
     def flux_in(i):
         arrive(*flux_pair(i))
         return jnp.concatenate(unpack(hr.at[i, 1], hr.at[i, 0], HALF), axis=1)
 
     def fold(x):
-        x = x[:, 0:128] + x[:, 128:256] + x[:, 256:384]
         total = x[0:8]
-        for i in range(1, ROWS // 8):
+        for i in range(1, x.shape[0] // 8):
             total = total + x[8 * i : 8 * i + 8]
         return total
+
+    def fold_wide(x):
+        return fold(x[:, 0:128] + x[:, 128:256] + x[:, 256:384])
 
     def all_copy(i, off):
         return pltpu.make_async_remote_copy(
@@ -374,10 +369,13 @@
             device_id={"space": lax.rem(me + off, n)}, device_id_type=MESH,
         )
 
-    def send_products(i, x, coupled, gam, z):
-        weight = wide(scale[1])
-        norm = jnp.sum(fold(x * x * weight), axis=0, keepdims=True)
-        product = jnp.sum(fold((x * coupled - 2.0 * gam * z) * weight), axis=0, keepdims=True)
+    def send_products(i, x, rest, outside):
+        weight = scale[1]
+        packed = jnp.concatenate([weight[0:LIVE], halves(weight[:HALF], weight[HALF:])], axis=0)
+        weight = wide(weight)
+        norm = jnp.sum(fold_wide(x * x * weight), axis=0, keepdims=True)
+        product = fold_wide(x * rest * weight) - 2.0 * fold(outside * packed)
+        product = jnp.sum(product, axis=0, keepdims=True)
         allb[i, me] = halves(norm + swap(norm), product + swap(product))
 
         def go(off, c):
@@ -399,39 +397,56 @@
             jnp.sum(jnp.where(left, 0.0, total), keepdims=True),
         )
 
-    def couple_neighbours(z, coupled):
-        spread(z)
-        qb[...] += coupled - joined(z, lam, lamx)
-
-    send_flux(0, gamb)
+    split_to(xs, gamb[...])
+    h, l = split2(lam[...])
+    xs[2 * ROWS : 2 * ROWS + 16] = h
+    xs[2 * ROWS + 16 : 2 * ROWS + 32] = l
+    flux, toward = flux_and_weights(AWAY)
+    pack(ts.at[0], ts.at[1], toward[:, 0:128], toward[:, 128:256], toward[:, 256:384])
+    send(*t_pair)
+    send_flux(0, flux)
+    flux, toward = flux_and_weights(OWN)
+    backb[...] = -flux
+    inner = edges(ext, OWN, nt)
     ones = jnp.ones((16, 768), BF16)
     row_total = (nt(ones, whi[...]) + nt(ones, wlo[...]))[0:1]
     arrive(*t_pair)
     came = jnp.concatenate(unpack(tr.at[1], tr.at[0], 8), axis=1)
-    dmode[...] += came + row_total * lam[...] + jnp.where(
+    dmode[...] = toward + came + row_total * lam[...] + jnp.where(
         lax.broadcasted_iota(jnp.int32, (16, nodes), 0) == 8, cap, 0.0
     )
     dmodex[...] = expanded(dmode)
     cplb[...] = joined(fieldb[...], dmode, dmodex)
-    zb[...] = neighbours(0, fieldb[...])
-    send_products(0, fieldb[...], cplb[...], gamb[...], zb[...])
-    couple_neighbours(zb[...], cplb[...])
-    imageb[...] = qb[...] - flux_in(0)
+    arrive(*pair(fs.at[0], fr.at[0], 0))
+    send_products(
+        0, fieldb[...], cplb[...] + 2.0 * backb[...], hs[0, 0] * fr[0, 0] + hs[0, 1] * fr[0, 1]
+    )
+    z = inner + outer(0)
+    split_to(xs, z)
+    spread(xs[0 : 2 * ROWS])
+    imageb[...] = cplb[...] + backb[...] - joined(z, lam, lamx)
+    imageb[...] -= flux_in(0)
     send_field(1, imageb[...])
 
-    spread(imageb[...])
-    gamq[...] = joined(imageb[...], lam, lamx)
+    split_to(ext, imageb[...], OWN)
+    spread(ext[:, OWN])
+    split_to(xs, joined(imageb[...], lam, lamx))
+    send_flux(1, edges(xs, AWAY, nn))
     cplq[...] = joined(imageb[...], dmode, dmodex)
-    send_flux(1, gamq)
-    z = neighbours(1, imageb[...])
+    backq[...] = -edges(xs, OWN, nn)
+    inner = edges(ext, OWN, nt)
     norm0, product0 = products(0)
     step0 = norm0 / product0
     r1b[...] = fieldb[...] - step0 * imageb[...]
-    send_products(
-        1, r1b[...], cplb[...] - step0 * cplq[...], gamb[...] - step0 * gamq[...],
-        zb[...] - step0 * z,
-    )
-    couple_neighbours(z, cplq[...])
+    cplb[...] = (cplb[...] + 2.0 * backb[...]) - step0 * (cplq[...] + 2.0 * backq[...])
+    arrive(*pair(fs.at[1], fr.at[1], 1))
+    outside = (hs[0, 0] - step0 * hs[1, 0]) * (fr[0, 0] - step0 * fr[1, 0])
+    outside += (hs[0, 1] - step0 * hs[1, 1]) * (fr[0, 1] - step0 * fr[1, 1])
+    send_products(1, r1b[...], cplb[...], outside)
+    z = inner + outer(1)
+    split_to(xs, z)
+    spread(xs[0 : 2 * ROWS])
+    cplq[...] = cplq[...] + backq[...] - joined(z, lam, lamx)
 
     def put_back(x):
         tiles = reorder([x[:, t * 128 : (t + 1) * 128] for t in range(3)], place)
@@ -447,7 +462,7 @@
     step1 = norm1 / (product1 - ratio * norm1 / step0)
     put_out(x_ref, (step0 + step1 * ratio) * inp[0:ROWS] + step1 * fieldb[...])
     gamb[...] = fieldb[...] - (step1 * (1.0 + ratio) / step0) * (inp[0:ROWS] - fieldb[...])
-    second = qb[...] - flux_in(1)
+    second = cplq[...] - flux_in(1)
     put_out(r_ref, gamb[...] + (step1 * step0) * put_back(second))
 
     for i in range(2):
@@ -493,7 +508,7 @@
             pltpu.VMEM((2 * ROWS + 32, nodes), BF16),
             pltpu.VMEM((2 * ROWS, 2 * nodes), BF16),
             small, pltpu.VMEM((384, nodes), F32), small, pltpu.VMEM((384, nodes), F32), small,
-            field, field, field, field, field, field, field, field, field,
+            field, field, field, field, field, field, field, field,
             message, message, message, message,
             pltpu.VMEM((2, 24, 128), F32),
             pltpu.VMEM((2, 24, 128), F32),

time: 28.4 us -> 27.3 us (0.961)
  Pallas kernels: 26.2 us -> 25.1 us
    pallas_call x1, Pallas kernels: 26.2 us -> 25.1 us  [shards(): pl.pallas_call(functools.partial(kernel, n), out_shape=(pltpu.VMEM((terms...]
where the time goes in v3:
time: 27.3 us; the launch traced here: 27.1 us
  Pallas kernels  25.1 us (92%)
  local copies, waits for them, and re-layouts  1.4 us (5%)
  between operations  0.64 us (2%)
    pallas_call x1, Pallas kernels, shards(): pl.pallas_call(functools.partial(kernel, n), out_shape=(pltpu.VMEM((terms...  25.1 us
    unnamed x2, local copies, waits for them, and re-layouts  1.4 us

profile of v3, /device:TPU:0, one launch (start us, length us, event | category | flops | bytes accessed | tf_op | source)
XLA Modules:
  0.0 27.1 jit_solution(4114832713658812492)
XLA Ops:
  0.6 25.1 %galerkin_cg.1 = (f32[165,384]{1,0:T(8,128)S(1)}, f32[165,384]{1,0:T(8,128)S(1)}) custom-call(f32[165,384]{1,0:T(8,128)} %rhs_hbm.1, f32[8,384]{1,0:T(8,128)} %var_hbm.1, f32[384]{0:T(512)} %cap_hbm.1, s32[6,23]{1,0:T(8,128)} %cols_hbm.1, s32[1,2,3]{2,1,0:T(2,128)} %list_hbm.1, bf16[768,352]{1,0:T(8,128)(2,1)} %constant.6.clone.coup_hbm, ...), custom_call_target="tpu_custom_call" | custom-call | tf_op jit(solution)/shard_map/galerkin_cg/pallas_call | solution.py:483
  25.7 0.7 %copy.13 = f32[165,384]{1,0:T(8,128)} copy(f32[165,384]{1,0:T(8,128)S(1)} %get-tuple-element.2) | data formatting | bytes 506880
  26.4 0.7 %copy.14 = f32[165,384]{1,0:T(8,128)} copy(f32[165,384]{1,0:T(8,128)S(1)} %get-tuple-element.3) | data formatting | bytes 506880

commit v4 on v3

--- a/solution.py
+++ b/solution.py
@@ -13,10 +13,10 @@
 ORDER = 3
 ITERS = 2
 SPREAD = 0.14
-ROWS = 176
-LOW, GAP, DEEP, LIVE = 45, 3, 48, 168
+ROWS, EVEN, ODD, DEEP = 176, 40, 48, 56
+PLACES = ((0, 1, 36), (1, 9, 48), (9, 45, 0), (45, 165, 56))
 HALF = ROWS // 2
-MSG = LIVE + HALF
+MSG = ROWS + HALF
 OWN, AWAY = slice(0, 384), slice(384, 768)
 MESH = pl.DeviceIdType.MESH
 F32 = jnp.float32
@@ -35,8 +35,12 @@
 
     grow([], ORDER)
     entries.sort(key=lambda m: (sum(m), tuple(-v for v in m)))
-    lookup = {m: i if i < LOW else i + GAP for i, m in enumerate(entries)}
-    coupling = np.zeros((768, 2 * ROWS), np.float32)
+    lookup = {}
+    for first, end, row in PLACES:
+        for i in range(first, end):
+            lookup[entries[i]] = row + i - first
+    even = np.zeros((VARS * EVEN, 2 * (ROWS - ODD)), np.float32)
+    odd = np.zeros((432, 2 * ODD), np.float32)
     expand = np.zeros((384, 16), np.float32)
     scale = np.ones((ROWS,), np.float64)
     for m, i in lookup.items():
@@ -45,18 +49,20 @@
         for k in range(VARS):
             lowered = lookup.get(m[:k] + (m[k] - 1,) + m[k + 1 :])
             raised = lookup.get(m[:k] + (m[k] + 1,) + m[k + 1 :])
-            for shift in (0, ROWS):
-                if i < DEEP:
-                    if lowered is not None:
-                        coupling[DEEP * k + i, shift + lowered] = m[k]
-                    coupling[DEEP * k + i, shift + raised] = 1.0
-                elif m[k] > 0:
+            for other, weight in ((lowered, m[k]), (raised, 1.0)):
+                if other is None:
+                    continue
+                if i < EVEN:
+                    even[EVEN * k + i, [other - ODD, ROWS - ODD + other - ODD]] = weight
+                elif i < DEEP:
+                    odd[8 * k + i - ODD, [other, ODD + other]] = weight
+                else:
                     place = 120 * held.index(k) + i - DEEP
-                    coupling[384 + place, shift + lowered] = m[k]
+                    odd[64 + place, [other, ODD + other]] = weight
                     expand[place, k] = 1.0
     scales = np.stack([scale, 1.0 / scale**2, 1.0 / scale], 0)
     scales = np.broadcast_to(scales[:, :, None], (3, ROWS, 128)).astype(np.float32)
-    return coupling, expand, scales
+    return even, odd, expand, scales
 
 
 def split2(x):
@@ -89,9 +95,9 @@
 
 def kernel(
     n,
-    rhs_hbm, var_hbm, cap_hbm, cols_hbm, list_hbm, coup_hbm, expand_hbm, scale_hbm, base_hbm,
+    rhs_hbm, var_hbm, cap_hbm, cols_hbm, list_hbm, even_hbm, odd_hbm, expand_hbm, scale_hbm, base_hbm,
     x_ref, r_ref,
-    rhs, var, capv, colv, lists, coup, expand, scale, base,
+    rhs, var, capv, colv, lists, even, odd, expand, scale, base,
     inp, blk, wc, wf, whi, wlo, ybuf, xs, ext, lam, lamx, dmode, dmodex, caps,
     fieldb, gamb, cplb, backb, imageb, cplq, backq, r1b,
     fs, fr, hs, hr, ts, tr, allb,
@@ -106,7 +112,8 @@
         for i, (src, dst) in enumerate(
             (
                 (list_hbm, lists), (rhs_hbm, rhs), (var_hbm, var), (cap_hbm, capv),
-                (cols_hbm, colv), (scale_hbm, scale), (coup_hbm, coup), (expand_hbm, expand),
+                (cols_hbm, colv), (scale_hbm, scale), (even_hbm, even), (odd_hbm, odd),
+                (expand_hbm, expand),
             )
         )
     ]
@@ -214,8 +221,8 @@
         for t in range(1, 6):
             at = jnp.where(perm[t] == r, jnp.int32(t), at)
         place.append(at)
-    inp[0:LOW] = rhs[0:LOW]
-    inp[DEEP:LIVE] = rhs[LOW:terms]
+    for first, end, row in PLACES:
+        inp[row : row + end - first] = rhs[first:end]
     inp[ROWS : ROWS + 8] = var[...]
     inp[ROWS + 8 : ROWS + 9] = capv[...].reshape(1, nodes)
 
@@ -251,17 +258,25 @@
         dst[0:ROWS, cols] = h
         dst[ROWS : 2 * ROWS, cols] = l
 
-    def spread(x):
-        ybuf[...] = nn(coup[...], x)
+    def spread(src):
+        cols = OWN
+        up = jnp.concatenate([src[ODD:ROWS, cols], src[ROWS + ODD : 2 * ROWS, cols]], axis=0)
+        down = jnp.concatenate([src[0:ODD, cols], src[ROWS : ROWS + ODD, cols]], axis=0)
+        ybuf[0 : VARS * EVEN] = nn(even[...], up)
+        ybuf[VARS * EVEN :] = nn(odd[...], down)
 
     def joined(x, w, wx):
-        top = w[8:9] * x[0:DEEP]
+        top = w[8:9] * x[0:EVEN]
+        one = w[8:9] * x[ODD:DEEP]
+        low = w[8:9] * x[DEEP:ROWS]
+        ones_at = VARS * EVEN
         for k in range(VARS):
-            top = top + w[k : k + 1] * ybuf[DEEP * k : DEEP * (k + 1)]
-        low = w[8:9] * x[DEEP:LIVE]
+            top = top + w[k : k + 1] * ybuf[EVEN * k : EVEN * (k + 1)]
+            one = one + w[k : k + 1] * ybuf[ones_at + 8 * k : ones_at + 8 * (k + 1)]
+        deep_at = ones_at + 64
         for s in range(3):
-            low = low + wx[120 * s : 120 * s + 120] * ybuf[384 + 120 * s : 504 + 120 * s]
-        return jnp.concatenate([top, low, jnp.zeros((ROWS - LIVE, nodes), F32)], axis=0)
+            low = low + wx[120 * s : 120 * s + 120] * ybuf[deep_at + 120 * s : deep_at + 120 * s + 120]
+        return jnp.concatenate([top, jnp.zeros((ODD - EVEN, nodes), F32), one, low], axis=0)
 
     def expanded(w):
         h, m, l = split3(w[...])
@@ -270,9 +285,10 @@
 
     ins[6].wait()
     ins[7].wait()
+    ins[8].wait()
     lamx[...] = expanded(lam)
     split_to(ext, fieldb[...], OWN)
-    spread(ext[:, OWN])
+    spread(ext)
     gamb[...] = joined(fieldb[...], lam, lamx)
 
     rowsc, rowse = wc.shape[0], base.shape[0]
@@ -371,7 +387,7 @@
 
     def send_products(i, x, rest, outside):
         weight = scale[1]
-        packed = jnp.concatenate([weight[0:LIVE], halves(weight[:HALF], weight[HALF:])], axis=0)
+        packed = jnp.concatenate([weight, halves(weight[:HALF], weight[HALF:])], axis=0)
         weight = wide(weight)
         norm = jnp.sum(fold_wide(x * x * weight), axis=0, keepdims=True)
         product = fold_wide(x * rest * weight) - 2.0 * fold(outside * packed)
@@ -423,13 +439,13 @@
     )
     z = inner + outer(0)
     split_to(xs, z)
-    spread(xs[0 : 2 * ROWS])
+    spread(xs)
     imageb[...] = cplb[...] + backb[...] - joined(z, lam, lamx)
     imageb[...] -= flux_in(0)
     send_field(1, imageb[...])
 
     split_to(ext, imageb[...], OWN)
-    spread(ext[:, OWN])
+    spread(ext)
     split_to(xs, joined(imageb[...], lam, lamx))
     send_flux(1, edges(xs, AWAY, nn))
     cplq[...] = joined(imageb[...], dmode, dmodex)
@@ -445,7 +461,7 @@
     send_products(1, r1b[...], cplb[...], outside)
     z = inner + outer(1)
     split_to(xs, z)
-    spread(xs[0 : 2 * ROWS])
+    spread(xs)
     cplq[...] = cplq[...] + backq[...] - joined(z, lam, lamx)
 
     def put_back(x):
@@ -453,8 +469,8 @@
         return jnp.concatenate([tile * scale[2] for tile in tiles], axis=1)
 
     def put_out(ref, y):
-        ref[0:LOW] = y[0:LOW]
-        ref[LOW:terms] = y[DEEP:LIVE]
+        for first, end, row in PLACES:
+            ref[first:end] = y[row : row + end - first]
 
     fieldb[...] = put_back(r1b[...])
     norm1, product1 = products(1)
@@ -475,7 +491,7 @@
     n = lax.axis_size("space")
     terms, nodes = right_side.shape
     blocks, slots, area = base_cond.shape
-    coupling, expand, scales = chaos_tables()
+    even, odd, expand, scales = chaos_tables()
     vmem = pl.BlockSpec(memory_space=pltpu.VMEM)
     field = pltpu.VMEM((ROWS, nodes), F32)
     small = pltpu.VMEM((16, nodes), F32)
@@ -486,7 +502,7 @@
             pltpu.VMEM((terms, nodes), F32),
             pltpu.VMEM((terms, nodes), F32),
         ),
-        in_specs=[pl.BlockSpec(memory_space=pltpu.HBM)] * 9,
+        in_specs=[pl.BlockSpec(memory_space=pltpu.HBM)] * 10,
         out_specs=(vmem, vmem),
         scratch_shapes=[
             pltpu.VMEM((terms, nodes), F32),
@@ -494,7 +510,8 @@
             pltpu.VMEM(capacity.shape, F32),
             pltpu.VMEM(block_cols.shape, jnp.int32),
             pltpu.SMEM(send_list.shape, jnp.int32),
-            pltpu.VMEM(coupling.shape, BF16),
+            pltpu.VMEM(even.shape, BF16),
+            pltpu.VMEM(odd.shape, BF16),
             pltpu.VMEM(expand.shape, BF16),
             pltpu.VMEM(scales.shape, F32),
             pltpu.VMEM((blocks * slots, area), F32),
@@ -504,7 +521,7 @@
             pltpu.VMEM((8 * nodes + 8, 128), F32),
             pltpu.VMEM((nodes, 2 * nodes), BF16),
             pltpu.VMEM((nodes, 2 * nodes), BF16),
-            pltpu.VMEM((768, nodes), F32),
+            pltpu.VMEM((VARS * EVEN + 432, nodes), F32),
             pltpu.VMEM((2 * ROWS + 32, nodes), BF16),
             pltpu.VMEM((2 * ROWS, 2 * nodes), BF16),
             small, pltpu.VMEM((384, nodes), F32), small, pltpu.VMEM((384, nodes), F32), small,
@@ -513,7 +530,7 @@
             pltpu.VMEM((2, 24, 128), F32),
             pltpu.VMEM((2, 24, 128), F32),
             pltpu.VMEM((2, n, 1, 128), F32),
-            pltpu.SemaphoreType.DMA((8,)),
+            pltpu.SemaphoreType.DMA((9,)),
             pltpu.SemaphoreType.DMA((4,)),
             pltpu.SemaphoreType.DMA((10,)),
             pltpu.SemaphoreType.DMA((10,)),
@@ -526,7 +543,7 @@
         name="galerkin_cg",
     )(
         right_side, var_field, capacity, block_cols, send_list,
-        jnp.asarray(coupling, BF16), jnp.asarray(expand, BF16), jnp.asarray(scales),
+        jnp.asarray(even, BF16), jnp.asarray(odd, BF16), jnp.asarray(expand, BF16), jnp.asarray(scales),
         base_cond.reshape(blocks * slots, area),
     )
 

time: 27.3 us -> 27.3 us (level)
  no operation moved by 1% of the time
where the time goes in v4:
time: 27.3 us; the launch traced here: 27.2 us
  Pallas kernels  25.1 us (92%)
  local copies, waits for them, and re-layouts  1.4 us (5%)
  between operations  0.64 us (2%)
    pallas_call x1, Pallas kernels, shards(): pl.pallas_call(functools.partial(kernel, n), out_shape=(pltpu.VMEM((terms...  25.1 us
    unnamed x2, local copies, waits for them, and re-layouts  1.4 us

profile of v4, /device:TPU:0, one launch (start us, length us, event | category | flops | bytes accessed | tf_op | source)
XLA Modules:
  0.0 27.2 jit_solution(15357808968166952991)
XLA Ops:
  0.6 25.1 %galerkin_cg.1 = (f32[165,384]{1,0:T(8,128)S(1)}, f32[165,384]{1,0:T(8,128)S(1)}) custom-call(f32[165,384]{1,0:T(8,128)} %rhs_hbm.1, f32[8,384]{1,0:T(8,128)} %var_hbm.1, f32[384]{0:T(512)} %cap_hbm.1, s32[6,23]{1,0:T(8,128)} %cols_hbm.1, s32[1,2,3]{2,1,0:T(2,128)} %list_hbm.1, bf16[320,256]{1,0:T(8,128)(2,1)} %constant.8.clone.even_hbm, ...), custom_call_target="tpu_custom_call" | custom-call | tf_op jit(solution)/shard_map/galerkin_cg/pallas_call | solution.py:499
  25.8 0.7 %copy.14 = f32[165,384]{1,0:T(8,128)} copy(f32[165,384]{1,0:T(8,128)S(1)} %get-tuple-element.2) | data formatting | bytes 506880
  26.5 0.7 %copy.15 = f32[165,384]{1,0:T(8,128)} copy(f32[165,384]{1,0:T(8,128)S(1)} %get-tuple-element.3) | data formatting | bytes 506880

commit v5 on v4

--- a/solution.py
+++ b/solution.py
@@ -60,9 +60,10 @@
                     place = 120 * held.index(k) + i - DEEP
                     odd[64 + place, [other, ODD + other]] = weight
                     expand[place, k] = 1.0
-    scales = np.stack([scale, 1.0 / scale**2, 1.0 / scale], 0)
-    scales = np.broadcast_to(scales[:, :, None], (3, ROWS, 128)).astype(np.float32)
-    return even, odd, expand, scales
+    scales = np.stack([scale, 1.0 / scale**2], 0)
+    scales = np.broadcast_to(scales[:, :, None], (2, ROWS, 128)).astype(np.float32)
+    final = np.array([1.0 / scale[lookup[m]] for m in entries], np.float32)
+    return even, odd, expand, scales, final
 
 
 def split2(x):
@@ -441,8 +442,8 @@
     split_to(xs, z)
     spread(xs)
     imageb[...] = cplb[...] + backb[...] - joined(z, lam, lamx)
+    send_field(1, imageb[...])
     imageb[...] -= flux_in(0)
-    send_field(1, imageb[...])
 
     split_to(ext, imageb[...], OWN)
     spread(ext)
@@ -456,6 +457,7 @@
     r1b[...] = fieldb[...] - step0 * imageb[...]
     cplb[...] = (cplb[...] + 2.0 * backb[...]) - step0 * (cplq[...] + 2.0 * backq[...])
     arrive(*pair(fs.at[1], fr.at[1], 1))
+    fr[1] = fr[1] - hs[0]
     outside = (hs[0, 0] - step0 * hs[1, 0]) * (fr[0, 0] - step0 * fr[1, 0])
     outside += (hs[0, 1] - step0 * hs[1, 1]) * (fr[0, 1] - step0 * fr[1, 1])
     send_products(1, r1b[...], cplb[...], outside)
@@ -466,12 +468,13 @@
 
     def put_back(x):
         tiles = reorder([x[:, t * 128 : (t + 1) * 128] for t in range(3)], place)
-        return jnp.concatenate([tile * scale[2] for tile in tiles], axis=1)
+        return jnp.concatenate(tiles, axis=1)
 
     def put_out(ref, y):
         for first, end, row in PLACES:
             ref[first:end] = y[row : row + end - first]
 
+    inp[0:ROWS] = inp[0:ROWS] * wide(scale[0])
     fieldb[...] = put_back(r1b[...])
     norm1, product1 = products(1)
     ratio = norm1 / norm0
@@ -491,12 +494,12 @@
     n = lax.axis_size("space")
     terms, nodes = right_side.shape
     blocks, slots, area = base_cond.shape
-    even, odd, expand, scales = chaos_tables()
+    even, odd, expand, scales, final = chaos_tables()
     vmem = pl.BlockSpec(memory_space=pltpu.VMEM)
     field = pltpu.VMEM((ROWS, nodes), F32)
     small = pltpu.VMEM((16, nodes), F32)
     message = pltpu.VMEM((2, 2, MSG, 128), F32)
-    return pl.pallas_call(
+    scaled = pl.pallas_call(
         functools.partial(kernel, n),
         out_shape=(
             pltpu.VMEM((terms, nodes), F32),
@@ -546,6 +549,8 @@
         jnp.asarray(even, BF16), jnp.asarray(odd, BF16), jnp.asarray(expand, BF16), jnp.asarray(scales),
         base_cond.reshape(blocks * slots, area),
     )
+    final = jnp.asarray(final)[:, None]
+    return scaled[0] * final, scaled[1] * final
 
 
 def solution(mesh):

time: 27.3 us -> 25.8 us (0.945)
  local copies, waits for them, and re-layouts: 1.4 us -> 0.01 us
  Pallas kernels: 25.1 us -> 24.1 us
  other arithmetic: 0 us -> 0.91 us
    unnamed x2, local copies, waits for them, and re-layouts: 1.4 us -> 0.01 us
    pallas_call x1, Pallas kernels: 25.1 us -> 24.1 us  [shards(): pl.pallas_call(functools.partial(kernel, n), out_shape=(pltpu.VMEM((terms...]
    mul x0 -> x1, other arithmetic: none -> 0.91 us  [shards(): return (scaled[0] * final, scaled[1] * final)]
where the time goes in v5:
time: 25.8 us; the launch traced here: 25.6 us
  Pallas kernels  24.1 us (93%)
  other arithmetic  0.91 us (4%)
  between operations  0.66 us (3%)
    pallas_call x1, Pallas kernels, shards(): pl.pallas_call(functools.partial(kernel, n), out_shape=(pltpu.VMEM((terms...  24.1 us
    mul x1, other arithmetic, shards(): return (scaled[0] * final, scaled[1] * final)  0.91 us

profile of v5, /device:TPU:0, one launch (start us, length us, event | category | flops | bytes accessed | tf_op | source)
XLA Modules:
  0.0 25.6 jit_solution(15063856386543854399)
XLA Ops:
  0.6 0.0 copy-start
  0.6 24.1 %galerkin_cg.1 = (f32[165,384]{1,0:T(8,128)S(1)}, f32[165,384]{1,0:T(8,128)S(1)}) custom-call(f32[165,384]{1,0:T(8,128)} %rhs_hbm.1, f32[8,384]{1,0:T(8,128)} %var_hbm.1, f32[384]{0:T(512)} %cap_hbm.1, s32[6,23]{1,0:T(8,128)} %cols_hbm.1, s32[1,2,3]{2,1,0:T(2,128)} %list_hbm.1, bf16[320,256]{1,0:T(8,128)(2,1)} %constant.10.clone.even_hbm, ...), custom_call_target="tpu_custom_call" | custom-call | tf_op jit(solution)/shard_map/galerkin_cg/pallas_call | solution.py:502
  24.7 0.0 copy-done
  24.7 0.9 %broadcast_multiply_fusion = (f32[165,384]{1,0:T(8,128)}, f32[165,384]{1,0:T(8,128)}) fusion(f32[165,384]{1,0:T(8,128)S(1)} %get-tuple-element.5, f32[165]{0:T(256)S(1)} %copy-done, f32[165,384]{1,0:T(8,128)S(1)} %get-tuple-element.4), kind=kLoop, calls=%fused_computation | loop fusion | flops 126720 | bytes 1014420 | tf_op jit(solution)/shard_map/mul | solution.py:553
Async XLA Ops:
  0.6 24.1 %copy-start = (f32[165]{0:T(256)S(1)}, f32[165]{0:T(256)}, u32[]{:S(2)}) copy-start(f32[165]{0:T(256)} %constant.14.clone) | copy-start | bytes 1984

commit v6 on v5

--- a/solution.py
+++ b/solution.py
@@ -316,10 +316,14 @@
     ).astype(F32).astype(BF16)
     for i in range(4):
         base_copy(i).wait()
-        for j in range(2):
-            cols = slice(i * chunk + j * 512, i * chunk + j * 512 + 512)
-            h, l = split2(base[:, cols])
-            wc[:, cols] = nn(pick, h) + nn(pick, l)
+
+    def merge(j, c):
+        cols = pl.ds(pl.multiple_of(j * 512, 512), 512)
+        h, l = split2(base[:, cols])
+        wc[:, cols] = nn(pick, h) + nn(pick, l)
+        return c
+
+    lax.fori_loop(0, base.shape[1] // 512, merge, 0)
 
     def lay(j, c):
         cols = pl.ds(pl.multiple_of(j * 128, 128), 128)
@@ -331,10 +335,15 @@
         return c
 
     lax.fori_loop(0, 32, lay, 0, unroll=4)
-    for q in (3, 4, 5, 0, 1, 2):
-        h, l = split2(wf[q * (nodes + 1) : q * (nodes + 1) + nodes])
-        whi[:, q * 128 : (q + 1) * 128] = h
-        wlo[:, q * 128 : (q + 1) * 128] = l
+
+    def halve(q, c):
+        cols = pl.ds(pl.multiple_of(q * 128, 128), 128)
+        h, l = split2(wf[pl.ds(q * (nodes + 1), nodes)])
+        whi[:, cols] = h
+        wlo[:, cols] = l
+        return c
+
+    lax.fori_loop(0, 6, halve, 0)
 
     t_pair = (remote(ts.at[1], tr.at[0], 8, nxt), remote(ts.at[0], tr.at[1], 9, prev))
 

time: 25.8 us -> 26.5 us (1.027)
  Pallas kernels: 24.1 us -> 24.8 us
    pallas_call x1, Pallas kernels: 24.1 us -> 24.8 us  [shards(): pl.pallas_call(functools.partial(kernel, n), out_shape=(pltpu.VMEM((terms...]
where the time goes in v6:
time: 26.5 us; the launch traced here: 26.4 us
  Pallas kernels  24.8 us (94%)
  other arithmetic  0.91 us (3%)
  between operations  0.66 us (2%)
    pallas_call x1, Pallas kernels, shards(): pl.pallas_call(functools.partial(kernel, n), out_shape=(pltpu.VMEM((terms...  24.8 us
    mul x1, other arithmetic, shards(): return (scaled[0] * final, scaled[1] * final)  0.91 us

profile of v6, /device:TPU:0, one launch (start us, length us, event | category | flops | bytes accessed | tf_op | source)
XLA Modules:
  0.0 26.4 jit_solution(11280940687691233799)
XLA Ops:
  0.6 0.0 copy-start
  0.6 24.8 %galerkin_cg.1 = (f32[165,384]{1,0:T(8,128)S(1)}, f32[165,384]{1,0:T(8,128)S(1)}) custom-call(f32[165,384]{1,0:T(8,128)} %rhs_hbm.1, f32[8,384]{1,0:T(8,128)} %var_hbm.1, f32[384]{0:T(512)} %cap_hbm.1, s32[6,23]{1,0:T(8,128)} %cols_hbm.1, s32[1,2,3]{2,1,0:T(2,128)} %list_hbm.1, bf16[320,256]{1,0:T(8,128)(2,1)} %constant.10.clone.even_hbm, ...), custom_call_target="tpu_custom_call" | custom-call | tf_op jit(solution)/shard_map/galerkin_cg/pallas_call | solution.py:511
  25.5 0.0 copy-done
  25.5 0.9 %broadcast_multiply_fusion = (f32[165,384]{1,0:T(8,128)}, f32[165,384]{1,0:T(8,128)}) fusion(f32[165,384]{1,0:T(8,128)S(1)} %get-tuple-element.5, f32[165]{0:T(256)S(1)} %copy-done, f32[165,384]{1,0:T(8,128)S(1)} %get-tuple-element.4), kind=kLoop, calls=%fused_computation | loop fusion | flops 126720 | bytes 1014420 | tf_op jit(solution)/shard_map/mul | solution.py:562
Async XLA Ops:
  0.6 24.8 %copy-start = (f32[165]{0:T(256)S(1)}, f32[165]{0:T(256)}, u32[]{:S(2)}) copy-start(f32[165]{0:T(256)} %constant.14.clone) | copy-start | bytes 1984

commit v7 on v5

--- a/solution.py
+++ b/solution.py
@@ -322,7 +322,7 @@
             wc[:, cols] = nn(pick, h) + nn(pick, l)
 
     def lay(j, c):
-        cols = pl.ds(pl.multiple_of(j * 128, 128), 128)
+        cols = slice(j * 128, j * 128 + 128)
         for t in range(6):
             even = wc[t * 16 : t * 16 + 8, cols]
             odd = wc[t * 16 + 8 : t * 16 + 16, cols]
@@ -330,7 +330,8 @@
             wf[pl.ds(t * 64 + 2 * j + 1, 8, stride=nodes + 1), :] = halves(swap(even), odd)
         return c
 
-    lax.fori_loop(0, 32, lay, 0, unroll=4)
+    for j in range(32):
+        lay(j, 0)
     for q in (3, 4, 5, 0, 1, 2):
         h, l = split2(wf[q * (nodes + 1) : q * (nodes + 1) + nodes])
         whi[:, q * 128 : (q + 1) * 128] = h
@@ -435,14 +436,14 @@
     dmodex[...] = expanded(dmode)
     cplb[...] = joined(fieldb[...], dmode, dmodex)
     arrive(*pair(fs.at[0], fr.at[0], 0))
-    send_products(
-        0, fieldb[...], cplb[...] + 2.0 * backb[...], hs[0, 0] * fr[0, 0] + hs[0, 1] * fr[0, 1]
-    )
     z = inner + outer(0)
     split_to(xs, z)
     spread(xs)
     imageb[...] = cplb[...] + backb[...] - joined(z, lam, lamx)
     send_field(1, imageb[...])
+    send_products(
+        0, fieldb[...], cplb[...] + 2.0 * backb[...], hs[0, 0] * fr[0, 0] + hs[0, 1] * fr[0, 1]
+    )
     imageb[...] -= flux_in(0)
 
     split_to(ext, imageb[...], OWN)

time: 25.8 us -> 25.3 us (0.981)
  Pallas kernels: 24.1 us -> 23.6 us
    pallas_call x1, Pallas kernels: 24.1 us -> 23.6 us  [shards(): pl.pallas_call(functools.partial(kernel, n), out_shape=(pltpu.VMEM((terms...]
where the time goes in v7:
time: 25.3 us; the launch traced here: 25.1 us
  Pallas kernels  23.6 us (93%)
  other arithmetic  0.91 us (4%)
  between operations  0.66 us (3%)
    pallas_call x1, Pallas kernels, shards(): pl.pallas_call(functools.partial(kernel, n), out_shape=(pltpu.VMEM((terms...  23.6 us
    mul x1, other arithmetic, shards(): return (scaled[0] * final, scaled[1] * final)  0.91 us

profile of v7, /device:TPU:0, one launch (start us, length us, event | category | flops | bytes accessed | tf_op | source)
XLA Modules:
  0.0 25.1 jit_solution(17654423625759134115)
XLA Ops:
  0.6 0.0 copy-start
  0.6 23.6 %galerkin_cg.1 = (f32[165,384]{1,0:T(8,128)S(1)}, f32[165,384]{1,0:T(8,128)S(1)}) custom-call(f32[165,384]{1,0:T(8,128)} %rhs_hbm.1, f32[8,384]{1,0:T(8,128)} %var_hbm.1, f32[384]{0:T(512)} %cap_hbm.1, s32[6,23]{1,0:T(8,128)} %cols_hbm.1, s32[1,2,3]{2,1,0:T(2,128)} %list_hbm.1, bf16[320,256]{1,0:T(8,128)(2,1)} %constant.10.clone.even_hbm, ...), custom_call_target="tpu_custom_call" | custom-call | tf_op jit(solution)/shard_map/galerkin_cg/pallas_call | solution.py:503
  24.2 0.0 copy-done
  24.2 0.9 %broadcast_multiply_fusion = (f32[165,384]{1,0:T(8,128)}, f32[165,384]{1,0:T(8,128)}) fusion(f32[165,384]{1,0:T(8,128)S(1)} %get-tuple-element.5, f32[165]{0:T(256)S(1)} %copy-done, f32[165,384]{1,0:T(8,128)S(1)} %get-tuple-element.4), kind=kLoop, calls=%fused_computation | loop fusion | flops 126720 | bytes 1014420 | tf_op jit(solution)/shard_map/mul | solution.py:554
Async XLA Ops:
  0.6 23.6 %copy-start = (f32[165]{0:T(256)S(1)}, f32[165]{0:T(256)}, u32[]{:S(2)}) copy-start(f32[165]{0:T(256)} %constant.14.clone) | copy-start | bytes 1984
